TPU v7x, 512 devices: a whole 4x8x8 slice. The times are simulated.
512 devices in a mesh: elec: 64 (over x, y, core), therm: 8 (over z).
Axes of the slice: x: 4, y: 8, z: 8, core: 2. Of those that a mesh axis runs over, the one named last changes fastest.
Arguments:
- injected_amperage: bfloat16 [16384, 64, 128], P(('elec', 'therm')), may hold values from -6 to 6
- voltage_self_admittance: float32 [16384, 64], P(('elec', 'therm')), may hold values from 1.2 to 2.5
- voltage_coupling_tiles: bfloat16 [16384, 4, 64, 64], P(('elec', 'therm')), may hold values from -0.5 to 0.5
- voltage_partner_tile_ids: int32 [16384, 4], P(('elec', 'therm')), may hold values from 0 to 31
- interface_tiles_per_level: int32 [2048, 2], P(('elec', 'therm')), may hold values from 0 to 31
- interface_admittance: bfloat16 [4096, 64, 64], P(('elec', 'therm')), may hold values from -0.5 to 0.5
- warmth_receiver_layer: int32 [16384, 1], P(('elec', 'therm')), may hold values from 0 to 7; in each aligned block of 32 rows (0 to 31, 32 to 63, ...) at most 8 rows name the same one
- warmth_receiver_tile: int32 [16384], P(('elec', 'therm')), may hold values from 0 to 31
- warmth_values: bfloat16 [16384, 64, 128], P(('elec', 'therm')), may hold values from -4 to 4
- warmth_self_coefficient: float32 [16384, 64], P(('elec', 'therm')), may hold values from 1 to 3
- warmth_coupling_tiles: bfloat16 [16384, 3, 64, 64], P(('elec', 'therm')), may hold values from -0.4375 to 0.4375
- warmth_partner_tile_ids: int32 [16384, 3], P(('elec', 'therm')), may hold values from 0 to 31
- layer_boundary_couplings: bfloat16 [2048, 64, 64], P(('elec', 'therm')), may hold values from -0.4375 to 0.4375
- substance_kind: int32 [16384, 64], P(('elec', 'therm')), may hold values from 0 to 7
- reference_material_kappas: float32 [8], replicated, may hold values from 0.5 to 4
- warmth_storage_per_point: float32 [16384, 64], P(('elec', 'therm')), may hold values from 1 to 4
Outputs:
- voltage_solution: bfloat16 [16384, 64, 128], P(('elec', 'therm'))
- advanced_warmth_values: float32 [16384, 64, 128], P(('elec', 'therm'))
Inputs may be any that keep to these rules, and one draw needn't show every extreme that they name: `warmth_receiver_layer`: among the 32 blocks of one device at most 8 name the same owner, and exactly 8 do for some owner. `voltage_partner_tile_ids`: indexes a block of the same device. `interface_tiles_per_level`: indexes a block of the same device. `warmth_receiver_tile`: indexes a thermal block of the owner. `warmth_partner_tile_ids`: indexes a thermal block of the same device.
All inputs are finite; a program needn't handle non-finite values.
Results may differ from a plain program's by a relative error of at most 0.025.
Values may be sent and summed in bfloat16 or wider, within the bound.
A program may use at most 64 MiB of HBM per device.

v0:
```python
import jax
import jax.numpy as jnp
from jax import lax
from jax.sharding import PartitionSpec as P

SWEEPS = 5
ZB = 2
relax_factor = 0.8
time_increment = 0.5


def from_partner(block, axis, bit):
    count = lax.axis_size(axis)
    route = []
    for low in range(count):
        high = low | 1 << bit
        if high != low and high < count:
            route += [(low, high), (high, low)]
    return lax.ppermute(block, axis, route)


def with_halo(x, sides, width):
    for axis, dim in sides:
        size, length = (lax.axis_size(axis), x.shape[dim])
        up = [(i, (i + 1) % size) for i in range(size - 1)]
        down = [(j, i) for i, j in up]
        last = lax.slice_in_dim(x, length - width, length, axis=dim)
        first = lax.slice_in_dim(x, 0, width, axis=dim)
        before = lax.ppermute(last, axis, up)
        after = lax.ppermute(first, axis, down)
        x = jnp.concatenate([before, x, after], axis=dim)
    return x


def near_product(field_b, near_blocks, near_index):
    picked = field_b[near_index]
    return jnp.einsum("rkab,rkbc->rac", near_blocks, picked, preferred_element_type=jnp.float32)


def electric_apply(
    field_b,
    voltage_self_admittance,
    voltage_coupling_tiles,
    voltage_partner_tile_ids,
    interface_tiles_per_level,
    interface_admittance,
):
    total = voltage_self_admittance[:, :, None] * field_b.astype(jnp.float32) + near_product(
        field_b, voltage_coupling_tiles, voltage_partner_tile_ids
    )
    received = []
    for level_bit in range(interface_tiles_per_level.shape[0]):
        outgoing = field_b[interface_tiles_per_level[level_bit]]
        received.append(from_partner(outgoing, "elec", level_bit))
    incoming = jnp.concatenate(received, axis=0)
    face_terms = jnp.einsum(
        "sab,sbc->sac", interface_admittance, incoming, preferred_element_type=jnp.float32
    )
    targets = interface_tiles_per_level.reshape(-1)
    selector = (targets[None, :] == jnp.arange(field_b.shape[0])[:, None]).astype(jnp.float32)
    spread = jnp.dot(
        selector, face_terms.reshape(face_terms.shape[0], -1), precision=lax.Precision.HIGHEST
    )
    return total + spread.reshape(total.shape)


def body(
    injected_amperage,
    voltage_self_admittance,
    voltage_coupling_tiles,
    voltage_partner_tile_ids,
    interface_tiles_per_level,
    interface_admittance,
    warmth_receiver_layer,
    warmth_receiver_tile,
    warmth_values,
    warmth_self_coefficient,
    warmth_coupling_tiles,
    warmth_partner_tile_ids,
    layer_boundary_couplings,
    substance_kind,
    reference_material_kappas,
    warmth_storage_per_point,
):
    source = injected_amperage.astype(jnp.float32)
    potential_f = relax_factor * source / voltage_self_admittance[:, :, None]
    for sweep_index in range(SWEEPS - 1):
        field_b = potential_f.astype(jnp.bfloat16)
        image = electric_apply(
            field_b,
            voltage_self_admittance,
            voltage_coupling_tiles,
            voltage_partner_tile_ids,
            interface_tiles_per_level,
            interface_admittance,
        )
        potential_f = (
            potential_f + relax_factor * (source - image) / voltage_self_admittance[:, :, None]
        )
    voltage_solution = potential_f.astype(jnp.bfloat16)
    current = electric_apply(
        voltage_solution,
        voltage_self_admittance,
        voltage_coupling_tiles,
        voltage_partner_tile_ids,
        interface_tiles_per_level,
        interface_admittance,
    )
    heat_b = (voltage_solution.astype(jnp.float32) * current).astype(jnp.bfloat16)
    owners = warmth_receiver_layer[:, 0]
    warmth_tile_count = warmth_values.shape[0]
    block_ids = jnp.arange(warmth_tile_count)[:, None]
    own_index = lax.axis_index("therm")
    heat_piece = lax.all_gather(heat_b, "therm", axis=0, tiled=True)
    owner_piece = lax.all_gather(owners, "therm", axis=0, tiled=True)
    row_piece = lax.all_gather(warmth_receiver_tile, "therm", axis=0, tiled=True)
    selector = ((row_piece[None, :] == block_ids) & (owner_piece[None, :] == own_index)).astype(
        jnp.bfloat16
    )
    resistive_dissipation = jnp.einsum(
        "jr,rbc->jbc", selector, heat_piece, preferred_element_type=jnp.float32
    )
    warmth_distribution = warmth_values.astype(jnp.float32)
    material_hits = (
        substance_kind[:, :, None] == jnp.arange(reference_material_kappas.shape[0])[None, None, :]
    ).astype(jnp.float32)
    pass_along = jnp.sum(material_hits * reference_material_kappas[None, None, :], axis=2)
    diffusivity_coefficient = pass_along[:, :, None] * (1.0 + 0.4 * jnp.tanh(warmth_distribution))
    stream_flow_second = (diffusivity_coefficient * warmth_distribution).astype(jnp.bfloat16)
    padded = with_halo(stream_flow_second, (("therm", 0),), ZB)
    below = padded[:ZB]
    above = padded[padded.shape[0] - ZB :]
    warmth_spread_operator = warmth_self_coefficient[:, :, None] * stream_flow_second.astype(
        jnp.float32
    ) + near_product(stream_flow_second, warmth_coupling_tiles, warmth_partner_tile_ids)
    low_terms = jnp.einsum(
        "zab,zbc->zac", layer_boundary_couplings[:ZB], below, preferred_element_type=jnp.float32
    )
    high_terms = jnp.einsum(
        "zab,zbc->zac", layer_boundary_couplings[ZB:], above, preferred_element_type=jnp.float32
    )
    warmth_spread_operator = (
        warmth_spread_operator.at[:ZB].add(low_terms).at[warmth_tile_count - ZB :].add(high_terms)
    )
    advanced_warmth_values = (
        warmth_distribution
        + time_increment
        * (resistive_dissipation - warmth_spread_operator)
        / warmth_storage_per_point[:, :, None]
    )
    return (voltage_solution, advanced_warmth_values)


def solution(mesh):
    return jax.shard_map(
        body,
        mesh=mesh,
        in_specs=(
            P(("elec", "therm"), None, None),
            P(("elec", "therm"), None),
            P(("elec", "therm"), None, None, None),
            P(("elec", "therm"), None),
            P(("elec", "therm"), None),
            P(("elec", "therm"), None, None),
            P(("elec", "therm"), None),
            P(("elec", "therm")),
            P(("elec", "therm"), None, None),
            P(("elec", "therm"), None),
            P(("elec", "therm"), None, None, None),
            P(("elec", "therm"), None),
            P(("elec", "therm"), None, None),
            P(("elec", "therm"), None),
            P(),
            P(("elec", "therm"), None),
        ),
        out_specs=(P(("elec", "therm"), None, None), P(("elec", "therm"), None, None)),
        check_vma=False,
    )
```

profile of v0, /device:TPU:1, one launch (start us, length us, event | category | flops | bytes accessed | tf_op | source)
XLA Modules:
  0.0 201.4 jit_solution(17127404310122124780)
XLA Ops:
  7.2 1.1 slice_reduce_fusion.3
  8.3 1.4 fusion.40
  10.3 8.3 %collective-permute-start.3 = (bf16[2,64,128]{2,1,0:T(8,128)(2,1)S(1)}, bf16[2,64,128]{2,1,0:T(8,128)(2,1)S(1)}, u32[]{:S(2)}, u32[]{:S(2)}) collective-permute-start(bf16[2,64,128]{2,1,0:T(8,128)(2,1)S(1)} %gather_fusion.4), channel_id=1, source_target_pairs={{0,64},{64,0},{8,72},{72,8},{16,80},{80,16},{24,88},{88,24},{32,96... | collective-permute-start | bytes 98312 | tf_op jit(solution)/shard_map/ppermute | solution.py:19
  19.2 2.4 %collective-permute-start.2 = (bf16[2,64,128]{2,1,0:T(8,128)(2,1)S(1)}, bf16[2,64,128]{2,1,0:T(8,128)(2,1)S(1)}, u32[]{:S(2)}, u32[]{:S(2)}) collective-permute-start(bf16[2,64,128]{2,1,0:T(8,128)(2,1)S(1)} %gather_fusion.3), channel_id=1, source_target_pairs={{0,32},{32,0},{8,40},{40,8},{16,48},{48,16},{24,56},{56,24},{64,96... | collective-permute-start | bytes 98312 | tf_op jit(solution)/shard_map/ppermute | solution.py:19
  22.2 2.3 %collective-permute-start.1 = (bf16[2,64,128]{2,1,0:T(8,128)(2,1)S(1)}, bf16[2,64,128]{2,1,0:T(8,128)(2,1)S(1)}, u32[]{:S(2)}, u32[]{:S(2)}) collective-permute-start(bf16[2,64,128]{2,1,0:T(8,128)(2,1)S(1)} %gather_fusion.2), channel_id=1, source_target_pairs={{0,16},{16,0},{8,24},{24,8},{32,48},{48,32},{40,56},{56,40},{64,80... | collective-permute-start | bytes 98312 | tf_op jit(solution)/shard_map/ppermute | solution.py:19
  25.1 3.4 %collective-permute-start = (bf16[2,64,128]{2,1,0:T(8,128)(2,1)S(1)}, bf16[2,64,128]{2,1,0:T(8,128)(2,1)S(1)}, u32[]{:S(2)}, u32[]{:S(2)}) collective-permute-start(bf16[2,64,128]{2,1,0:T(8,128)(2,1)S(1)} %gather_fusion.1), channel_id=1, source_target_pairs={{0,8},{8,0},{16,24},{24,16},{32,40},{40,32},{48,56},{56,48},{64,72... | collective-permute-start | bytes 98312 | tf_op jit(solution)/shard_map/ppermute | solution.py:19
  28.5 0.7 compare_select_fusion.1
  29.4 0.8 copy.74
  30.2 2.2 %gather_fusion = bf16[128,64,128]{2,1,0:T(8,128)(2,1)} fusion(bf16[32,64,128]{2,1,0:T(8,128)(2,1)S(1)} %fusion.40, s32[1024]{0:T(1024)S(1)} %pad_clamp_fusion.5), kind=kCustom, calls=%fused_computation | custom fusion | bytes 4194816 | tf_op jit(solution)/shard_map/gather | solution.py:36
  32.6 0.7 fusion.49
  33.3 4.2 %fusion.120 = (bf16[32,64,128]{2,1,0:T(8,128)(2,1)S(1)}, f32[32,64,128]{2,1,0:T(8,128)}) fusion(f32[32,64,128]{2,0,1:T(8,128)S(1)} %fusion.49, bf16[32,4,64,64]{3,2,1,0:T(8,128)(2,1)S(1)} %copy-done, bf16[32,4,64,128]{3,2,1,0:T(8,128)(2,1)} %bitcast.203, f32[32,64]{1,0:T(8,128)S(1)} %copy-done.3, bf16[32,64,128]{2,1,0:T(8,128)(2,1)} %param.20), kind=kOutput, calls=%fused_computation.184 | convolution fusion | flops 137625600 | bytes 6299648 | tf_op jit(solution)/shard_map/rkab,rkbc->rac/dot_general | solution.py:37
  39.8 5.7 %collective-permute-start.7 = (bf16[2,64,128]{2,1,0:T(8,128)(2,1)S(1)}, bf16[2,64,128]{2,1,0:T(8,128)(2,1)S(1)}, u32[]{:S(2)}, u32[]{:S(2)}) collective-permute-start(bf16[2,64,128]{2,1,0:T(8,128)(2,1)S(1)} %gather_fusion.9), channel_id=1, source_target_pairs={{0,64},{64,0},{8,72},{72,8},{16,80},{80,16},{24,88},{88,24},{32,96... | collective-permute-start | bytes 98312 | tf_op jit(solution)/shard_map/ppermute | solution.py:19
  45.4 4.5 %collective-permute-start.6 = (bf16[2,64,128]{2,1,0:T(8,128)(2,1)S(1)}, bf16[2,64,128]{2,1,0:T(8,128)(2,1)S(1)}, u32[]{:S(2)}, u32[]{:S(2)}) collective-permute-start(bf16[2,64,128]{2,1,0:T(8,128)(2,1)S(1)} %gather_fusion.8), channel_id=1, source_target_pairs={{0,32},{32,0},{8,40},{40,8},{16,48},{48,16},{24,56},{56,24},{64,96... | collective-permute-start | bytes 98312 | tf_op jit(solution)/shard_map/ppermute | solution.py:19
  50.0 3.6 %collective-permute-start.5 = (bf16[2,64,128]{2,1,0:T(8,128)(2,1)S(1)}, bf16[2,64,128]{2,1,0:T(8,128)(2,1)S(1)}, u32[]{:S(2)}, u32[]{:S(2)}) collective-permute-start(bf16[2,64,128]{2,1,0:T(8,128)(2,1)S(1)} %gather_fusion.7), channel_id=1, source_target_pairs={{0,16},{16,0},{8,24},{24,8},{32,48},{48,32},{40,56},{56,40},{64,80... | collective-permute-start | bytes 98312 | tf_op jit(solution)/shard_map/ppermute | solution.py:19
  53.6 2.8 %collective-permute-start.4 = (bf16[2,64,128]{2,1,0:T(8,128)(2,1)S(1)}, bf16[2,64,128]{2,1,0:T(8,128)(2,1)S(1)}, u32[]{:S(2)}, u32[]{:S(2)}) collective-permute-start(bf16[2,64,128]{2,1,0:T(8,128)(2,1)S(1)} %gather_fusion.6), channel_id=1, source_target_pairs={{0,8},{8,0},{16,24},{24,16},{32,40},{40,32},{48,56},{56,48},{64,72... | collective-permute-start | bytes 98312 | tf_op jit(solution)/shard_map/ppermute | solution.py:19
  56.4 2.2 %gather_fusion.5 = bf16[128,64,128]{2,1,0:T(8,128)(2,1)} fusion(bf16[32,64,128]{2,1,0:T(8,128)(2,1)S(1)} %get-tuple-element.42, s32[1024]{0:T(1024)S(1)} %pad_clamp_fusion.5), kind=kCustom, calls=%fused_computation.5 | custom fusion | bytes 4194816 | tf_op jit(solution)/shard_map/gather | solution.py:36
  59.5 4.5 %fusion.121 = (bf16[32,64,128]{2,1,0:T(8,128)(2,1)S(1)}, f32[32,64,128]{2,1,0:T(8,128)}) fusion(f32[32,64,128]{2,1,0:T(8,128)} %get-tuple-element.43, f32[32,64,128]{2,0,1:T(8,128)S(1)} %fusion.47, bf16[32,4,64,64]{3,2,1,0:T(8,128)(2,1)S(1)} %copy-done, bf16[32,4,64,128]{3,2,1,0:T(8,128)(2,1)} %bitcast.201, ...), kind=kOutput, calls=%fused_computation.185 | convolution fusion | flops 136839168 | bytes 7872512 | tf_op jit(solution)/shard_map/rkab,rkbc->rac/dot_general | solution.py:37
  66.2 2.1 %collective-permute-start.11 = (bf16[2,64,128]{2,1,0:T(8,128)(2,1)S(1)}, bf16[2,64,128]{2,1,0:T(8,128)(2,1)S(1)}, u32[]{:S(2)}, u32[]{:S(2)}) collective-permute-start(bf16[2,64,128]{2,1,0:T(8,128)(2,1)S(1)} %gather_fusion.14), channel_id=1, source_target_pairs={{0,64},{64,0},{8,72},{72,8},{16,80},{80,16},{24,88},{88,24},{32,96... | collective-permute-start | bytes 98312 | tf_op jit(solution)/shard_map/ppermute | solution.py:19
  68.3 2.4 %collective-permute-start.10 = (bf16[2,64,128]{2,1,0:T(8,128)(2,1)S(1)}, bf16[2,64,128]{2,1,0:T(8,128)(2,1)S(1)}, u32[]{:S(2)}, u32[]{:S(2)}) collective-permute-start(bf16[2,64,128]{2,1,0:T(8,128)(2,1)S(1)} %gather_fusion.13), channel_id=1, source_target_pairs={{0,32},{32,0},{8,40},{40,8},{16,48},{48,16},{24,56},{56,24},{64,96... | collective-permute-start | bytes 98312 | tf_op jit(solution)/shard_map/ppermute | solution.py:19
  70.7 2.3 %collective-permute-start.9 = (bf16[2,64,128]{2,1,0:T(8,128)(2,1)S(1)}, bf16[2,64,128]{2,1,0:T(8,128)(2,1)S(1)}, u32[]{:S(2)}, u32[]{:S(2)}) collective-permute-start(bf16[2,64,128]{2,1,0:T(8,128)(2,1)S(1)} %gather_fusion.12), channel_id=1, source_target_pairs={{0,16},{16,0},{8,24},{24,8},{32,48},{48,32},{40,56},{56,40},{64,80... | collective-permute-start | bytes 98312 | tf_op jit(solution)/shard_map/ppermute | solution.py:19
  73.1 2.8 %collective-permute-start.8 = (bf16[2,64,128]{2,1,0:T(8,128)(2,1)S(1)}, bf16[2,64,128]{2,1,0:T(8,128)(2,1)S(1)}, u32[]{:S(2)}, u32[]{:S(2)}) collective-permute-start(bf16[2,64,128]{2,1,0:T(8,128)(2,1)S(1)} %gather_fusion.11), channel_id=1, source_target_pairs={{0,8},{8,0},{16,24},{24,16},{32,40},{40,32},{48,56},{56,48},{64,72... | collective-permute-start | bytes 98312 | tf_op jit(solution)/shard_map/ppermute | solution.py:19
  75.8 2.2 %gather_fusion.10 = bf16[128,64,128]{2,1,0:T(8,128)(2,1)} fusion(bf16[32,64,128]{2,1,0:T(8,128)(2,1)S(1)} %get-tuple-element.44, s32[1024]{0:T(1024)S(1)} %pad_clamp_fusion.5), kind=kCustom, calls=%fused_computation.10 | custom fusion | bytes 4194816 | tf_op jit(solution)/shard_map/gather | solution.py:36
  78.2 0.7 fusion.45
  78.9 4.5 %fusion.122 = (bf16[32,64,128]{2,1,0:T(8,128)(2,1)S(1)}, f32[32,64,128]{2,1,0:T(8,128)}) fusion(f32[32,64,128]{2,1,0:T(8,128)} %get-tuple-element.45, f32[32,64,128]{2,0,1:T(8,128)S(1)} %fusion.45, bf16[32,4,64,64]{3,2,1,0:T(8,128)(2,1)S(1)} %copy-done, bf16[32,4,64,128]{3,2,1,0:T(8,128)(2,1)} %bitcast.202, ...), kind=kOutput, calls=%fused_computation.186 | convolution fusion | flops 136839168 | bytes 7872512 | tf_op jit(solution)/shard_map/rkab,rkbc->rac/dot_general | solution.py:37
  85.7 5.9 %collective-permute-start.15 = (bf16[2,64,128]{2,1,0:T(8,128)(2,1)S(1)}, bf16[2,64,128]{2,1,0:T(8,128)(2,1)S(1)}, u32[]{:S(2)}, u32[]{:S(2)}) collective-permute-start(bf16[2,64,128]{2,1,0:T(8,128)(2,1)S(1)} %gather_fusion.19), channel_id=1, source_target_pairs={{0,64},{64,0},{8,72},{72,8},{16,80},{80,16},{24,88},{88,24},{32,96... | collective-permute-start | bytes 98312 | tf_op jit(solution)/shard_map/ppermute | solution.py:19
  91.5 4.3 %collective-permute-start.14 = (bf16[2,64,128]{2,1,0:T(8,128)(2,1)S(1)}, bf16[2,64,128]{2,1,0:T(8,128)(2,1)S(1)}, u32[]{:S(2)}, u32[]{:S(2)}) collective-permute-start(bf16[2,64,128]{2,1,0:T(8,128)(2,1)S(1)} %gather_fusion.18), channel_id=1, source_target_pairs={{0,32},{32,0},{8,40},{40,8},{16,48},{48,16},{24,56},{56,24},{64,96... | collective-permute-start | bytes 98312 | tf_op jit(solution)/shard_map/ppermute | solution.py:19
  95.9 3.6 %collective-permute-start.13 = (bf16[2,64,128]{2,1,0:T(8,128)(2,1)S(1)}, bf16[2,64,128]{2,1,0:T(8,128)(2,1)S(1)}, u32[]{:S(2)}, u32[]{:S(2)}) collective-permute-start(bf16[2,64,128]{2,1,0:T(8,128)(2,1)S(1)} %gather_fusion.17), channel_id=1, source_target_pairs={{0,16},{16,0},{8,24},{24,8},{32,48},{48,32},{40,56},{56,40},{64,80... | collective-permute-start | bytes 98312 | tf_op jit(solution)/shard_map/ppermute | solution.py:19
  99.5 2.9 %collective-permute-start.12 = (bf16[2,64,128]{2,1,0:T(8,128)(2,1)S(1)}, bf16[2,64,128]{2,1,0:T(8,128)(2,1)S(1)}, u32[]{:S(2)}, u32[]{:S(2)}) collective-permute-start(bf16[2,64,128]{2,1,0:T(8,128)(2,1)S(1)} %gather_fusion.16), channel_id=1, source_target_pairs={{0,8},{8,0},{16,24},{24,16},{32,40},{40,32},{48,56},{56,48},{64,72... | collective-permute-start | bytes 98312 | tf_op jit(solution)/shard_map/ppermute | solution.py:19
  102.5 2.2 %gather_fusion.15 = bf16[128,64,128]{2,1,0:T(8,128)(2,1)} fusion(bf16[32,64,128]{2,1,0:T(8,128)(2,1)S(1)} %get-tuple-element.46, s32[1024]{0:T(1024)S(1)} %pad_clamp_fusion.5), kind=kCustom, calls=%fused_computation.15 | custom fusion | bytes 4194816 | tf_op jit(solution)/shard_map/gather | solution.py:36
  105.5 3.5 %fusion.26 = bf16[32,64,128]{2,1,0:T(8,128)(2,1)S(1)} fusion(f32[32,64,128]{2,1,0:T(8,128)} %get-tuple-element.47, bf16[32,4,64,64]{3,2,1,0:T(8,128)(2,1)S(1)} %copy-done, bf16[32,4,64,128]{3,2,1,0:T(8,128)(2,1)} %bitcast.204, bf16[32,64,128]{2,1,0:T(8,128)(2,1)} %param.20, f32[32,64,128]{2,0,1:T(8,128)S(1)} %fusion.43, ...), kind=kOutput, calls=%fused_computation.63 | convolution fusion | flops 136839168 | bytes 6823936 | tf_op jit(solution)/shard_map/rkab,rkbc->rac/dot_general | solution.py:37
  111.3 2.1 %collective-permute-start.19 = (bf16[2,64,128]{2,1,0:T(8,128)(2,1)S(1)}, bf16[2,64,128]{2,1,0:T(8,128)(2,1)S(1)}, u32[]{:S(2)}, u32[]{:S(2)}) collective-permute-start(bf16[2,64,128]{2,1,0:T(8,128)(2,1)S(1)} %gather_fusion.24), channel_id=1, source_target_pairs={{0,64},{64,0},{8,72},{72,8},{16,80},{80,16},{24,88},{88,24},{32,96... | collective-permute-start | bytes 98312 | tf_op jit(solution)/shard_map/ppermute | solution.py:19
  113.4 2.4 %collective-permute-start.18 = (bf16[2,64,128]{2,1,0:T(8,128)(2,1)S(1)}, bf16[2,64,128]{2,1,0:T(8,128)(2,1)S(1)}, u32[]{:S(2)}, u32[]{:S(2)}) collective-permute-start(bf16[2,64,128]{2,1,0:T(8,128)(2,1)S(1)} %gather_fusion.23), channel_id=1, source_target_pairs={{0,32},{32,0},{8,40},{40,8},{16,48},{48,16},{24,56},{56,24},{64,96... | collective-permute-start | bytes 98312 | tf_op jit(solution)/shard_map/ppermute | solution.py:19
  115.8 2.3 %collective-permute-start.17 = (bf16[2,64,128]{2,1,0:T(8,128)(2,1)S(1)}, bf16[2,64,128]{2,1,0:T(8,128)(2,1)S(1)}, u32[]{:S(2)}, u32[]{:S(2)}) collective-permute-start(bf16[2,64,128]{2,1,0:T(8,128)(2,1)S(1)} %gather_fusion.22), channel_id=1, source_target_pairs={{0,16},{16,0},{8,24},{24,8},{32,48},{48,32},{40,56},{56,40},{64,80... | collective-permute-start | bytes 98312 | tf_op jit(solution)/shard_map/ppermute | solution.py:19
  118.2 2.8 %collective-permute-start.16 = (bf16[2,64,128]{2,1,0:T(8,128)(2,1)S(1)}, bf16[2,64,128]{2,1,0:T(8,128)(2,1)S(1)}, u32[]{:S(2)}, u32[]{:S(2)}) collective-permute-start(bf16[2,64,128]{2,1,0:T(8,128)(2,1)S(1)} %gather_fusion.21), channel_id=1, source_target_pairs={{0,8},{8,0},{16,24},{24,16},{32,40},{40,32},{48,56},{56,48},{64,72... | collective-permute-start | bytes 98312 | tf_op jit(solution)/shard_map/ppermute | solution.py:19
  120.9 2.2 %gather_fusion.20 = bf16[128,64,128]{2,1,0:T(8,128)(2,1)} fusion(bf16[32,64,128]{2,1,0:T(8,128)(2,1)S(1)} %fusion.26, s32[1024]{0:T(1024)S(1)} %pad_clamp_fusion.5), kind=kCustom, calls=%fused_computation.20 | custom fusion | bytes 4194816 | tf_op jit(solution)/shard_map/gather | solution.py:36
  124.0 3.9 %fusion.23 = bf16[32,64,128]{2,1,0:T(8,128)(2,1)} fusion(bf16[32,4,64,64]{3,2,1,0:T(8,128)(2,1)S(1)} %copy-done, bf16[32,4,64,128]{3,2,1,0:T(8,128)(2,1)} %bitcast.199, bf16[32,64,128]{2,1,0:T(8,128)(2,1)S(1)} %fusion.26, f32[32,64,128]{2,0,1:T(8,128)S(1)} %fusion.41, f32[32,64]{1,0:T(8,128)S(1)} %copy-done.3), kind=kOutput, calls=%fused_computation.60 | convolution fusion | flops 135790592 | bytes 5251072 | tf_op jit(solution)/shard_map/rkab,rkbc->rac/dot_general | solution.py:37
  128.7 4.0 %collective-permute-start.20 = (bf16[2,64,128]{2,0,1:T(2,128)(2,1)S(1)}, bf16[2,64,128]{2,0,1:T(2,128)(2,1)S(1)}, u32[]{:S(2)}, u32[]{:S(2)}) collective-permute-start(bf16[2,64,128]{2,0,1:T(2,128)(2,1)S(1)} %get-tuple-element.41), channel_id=1, source_target_pairs={{0,1},{1,2},{2,3},{3,4},{4,5},{5,6},{6,7},{8,9},{9,10},{10,11},{11... | collective-permute-start | bytes 98312 | tf_op jit(solution)/shard_map/ppermute | solution.py:29
  132.8 1.3 collective-permute-start.21
  134.6 2.0 gather_fusion.25
  136.6 1.3 dynamic-slice.18
  138.9 16.9 %all-reduce.2 = (s32[256]{0:T(256)S(1)}, s32[256]{0:T(256)S(1)}) all-reduce(s32[256]{0:T(256)S(1)} %dynamic-update-slice.6, s32[256]{0:T(256)S(1)} %bitcast_dynamic-update-slice_fusion), channel_id=1, replica_groups=mesh['elec'=64,'therm'=8] {'therm'}, use_global_device_ids=true, to_apply=%add | all-reduce | flops 512 | bytes 4096
  155.8 2.6 %convolution_bitcast_fusion = f32[32,128,64]{1,2,0:T(8,128)S(1)} fusion(bf16[32,3,64,64]{3,2,1,0:T(8,128)(2,1)} %param.30, bf16[32,3,64,128]{3,2,1,0:T(8,128)(2,1)} %bitcast.200), kind=kOutput, calls=%fused_computation.37 | convolution fusion | flops 100663296 | bytes 3407872 | tf_op jit(solution)/shard_map/rkab,rkbc->rac/dot_general | solution.py:37
  158.4 3.1 %bitcast_add_fusion = f32[32,64,128]{2,0,1:T(8,128)} fusion(f32[32,128,64]{1,2,0:T(8,128)S(1)} %convolution_bitcast_fusion, f32[32,64]{0,1:T(8,128)S(1)} %copy.82, bf16[32,64,128]{2,1,0:T(8,128)(2,1)S(1)} %copy-done.2, f32[32,64]{0,1:T(8,128)S(1)} %copy.83), kind=kLoop, calls=%fused_computation.80 | loop fusion | flops 2359296 | bytes 2637824 | tf_op jit(solution)/shard_map/add | solution.py:133
  161.9 1.7 fusion.87
  163.6 1.6 fusion.86
  165.2 22.6 %all-gather.3.cloned.1.call-done = bf16[256,64,128]{2,1,0:T(8,128)(2,1)} async-done(((bf16[32,64,128]{2,1,0:T(8,128)(2,1)}), bf16[256,64,128]{2,1,0:T(8,128)(2,1)}) %all-gather.3.cloned.1.call-update) | async-done | bytes 4194320 | tf_op jit(solution)/shard_map/all_gather | solution.py:114
  187.8 5.2 %convert_add_fusion = f32[32,64,128]{2,0,1:T(8,128)S(1)} fusion(f32[32,64,128]{2,0,1:T(8,128)} %fusion.86, bf16[256,64,128]{2,1,0:T(8,128)(2,1)} %all-gather.3.cloned.1.call-done, f32[32,64]{0,1:T(8,128)S(1)} %copy.91, bf16[32,64,128]{2,1,0:T(8,128)(2,1)S(1)} %copy-done.2, s32[256]{0:T(256)S(1)} %get-tuple-element.38, ...), kind=kOutput, calls=%fused_computation.33 | convolution fusion | flops 135544832 | bytes 6825216 | tf_op jit(solution)/shard_map/jr,rbc->jbc/dot_general | solution.py:120
  193.0 1.6 copy.92
  (106 shorter events, 16.5 us)
Async XLA Ops:
  7.2 26.1 %copy-start = (bf16[32,4,64,64]{3,2,1,0:T(8,128)(2,1)S(1)}, bf16[32,4,64,64]{3,2,1,0:T(8,128)(2,1)}, u32[]{:S(2)}) copy-start(bf16[32,4,64,64]{3,2,1,0:T(8,128)(2,1)} %param.22) | copy-start | bytes 3145732
  7.2 180.6 %all-gather.3.cloned.1.call-start = ((), (), s32[]{:S(2)}) async-start(), calls=%async_computation | async-start | bytes 4718592 | tf_op jit(solution)/shard_map/all_gather | solution.py:114
  10.3 22.1 %collective-permute-start.3 = (bf16[2,64,128]{2,1,0:T(8,128)(2,1)S(1)}, bf16[2,64,128]{2,1,0:T(8,128)(2,1)S(1)}, u32[]{:S(2)}, u32[]{:S(2)}) collective-permute-start(bf16[2,64,128]{2,1,0:T(8,128)(2,1)S(1)} %gather_fusion.4), channel_id=1, source_target_pairs={{0,64},{64,0},{8,72},{72,8},{16,80},{80,16},{24,88},{88,24},{32,96... | collective-permute-start | bytes 98312 | tf_op jit(solution)/shard_map/ppermute | solution.py:19
  19.2 13.3 %collective-permute-start.2 = (bf16[2,64,128]{2,1,0:T(8,128)(2,1)S(1)}, bf16[2,64,128]{2,1,0:T(8,128)(2,1)S(1)}, u32[]{:S(2)}, u32[]{:S(2)}) collective-permute-start(bf16[2,64,128]{2,1,0:T(8,128)(2,1)S(1)} %gather_fusion.3), channel_id=1, source_target_pairs={{0,32},{32,0},{8,40},{40,8},{16,48},{48,16},{24,56},{56,24},{64,96... | collective-permute-start | bytes 98312 | tf_op jit(solution)/shard_map/ppermute | solution.py:19
  22.2 10.2 %collective-permute-start.1 = (bf16[2,64,128]{2,1,0:T(8,128)(2,1)S(1)}, bf16[2,64,128]{2,1,0:T(8,128)(2,1)S(1)}, u32[]{:S(2)}, u32[]{:S(2)}) collective-permute-start(bf16[2,64,128]{2,1,0:T(8,128)(2,1)S(1)} %gather_fusion.2), channel_id=1, source_target_pairs={{0,16},{16,0},{8,24},{24,8},{32,48},{48,32},{40,56},{56,40},{64,80... | collective-permute-start | bytes 98312 | tf_op jit(solution)/shard_map/ppermute | solution.py:19
  25.1 7.4 %collective-permute-start = (bf16[2,64,128]{2,1,0:T(8,128)(2,1)S(1)}, bf16[2,64,128]{2,1,0:T(8,128)(2,1)S(1)}, u32[]{:S(2)}, u32[]{:S(2)}) collective-permute-start(bf16[2,64,128]{2,1,0:T(8,128)(2,1)S(1)} %gather_fusion.1), channel_id=1, source_target_pairs={{0,8},{8,0},{16,24},{24,16},{32,40},{40,32},{48,56},{56,48},{64,72... | collective-permute-start | bytes 98312 | tf_op jit(solution)/shard_map/ppermute | solution.py:19
  30.2 2.2 %copy-start.10 = (bf16[8,64,64]{2,1,0:T(8,128)(2,1)S(1)}, bf16[8,64,64]{2,1,0:T(8,128)(2,1)}, u32[]{:S(2)}) copy-start(bf16[8,64,64]{2,1,0:T(8,128)(2,1)} %param.25) | copy-start | bytes 196612
  30.2 3.1 %copy-start.3 = (f32[32,64]{1,0:T(8,128)S(1)}, f32[32,64]{1,0:T(8,128)}, u32[]{:S(2)}) copy-start(f32[32,64]{1,0:T(8,128)} %param.21) | copy-start | bytes 24580
  39.8 18.8 %collective-permute-start.7 = (bf16[2,64,128]{2,1,0:T(8,128)(2,1)S(1)}, bf16[2,64,128]{2,1,0:T(8,128)(2,1)S(1)}, u32[]{:S(2)}, u32[]{:S(2)}) collective-permute-start(bf16[2,64,128]{2,1,0:T(8,128)(2,1)S(1)} %gather_fusion.9), channel_id=1, source_target_pairs={{0,64},{64,0},{8,72},{72,8},{16,80},{80,16},{24,88},{88,24},{32,96... | collective-permute-start | bytes 98312 | tf_op jit(solution)/shard_map/ppermute | solution.py:19
  45.4 13.1 %collective-permute-start.6 = (bf16[2,64,128]{2,1,0:T(8,128)(2,1)S(1)}, bf16[2,64,128]{2,1,0:T(8,128)(2,1)S(1)}, u32[]{:S(2)}, u32[]{:S(2)}) collective-permute-start(bf16[2,64,128]{2,1,0:T(8,128)(2,1)S(1)} %gather_fusion.8), channel_id=1, source_target_pairs={{0,32},{32,0},{8,40},{40,8},{16,48},{48,16},{24,56},{56,24},{64,96... | collective-permute-start | bytes 98312 | tf_op jit(solution)/shard_map/ppermute | solution.py:19
  50.0 8.6 %collective-permute-start.5 = (bf16[2,64,128]{2,1,0:T(8,128)(2,1)S(1)}, bf16[2,64,128]{2,1,0:T(8,128)(2,1)S(1)}, u32[]{:S(2)}, u32[]{:S(2)}) collective-permute-start(bf16[2,64,128]{2,1,0:T(8,128)(2,1)S(1)} %gather_fusion.7), channel_id=1, source_target_pairs={{0,16},{16,0},{8,24},{24,8},{32,48},{48,32},{40,56},{56,40},{64,80... | collective-permute-start | bytes 98312 | tf_op jit(solution)/shard_map/ppermute | solution.py:19
  53.6 4.9 %collective-permute-start.4 = (bf16[2,64,128]{2,1,0:T(8,128)(2,1)S(1)}, bf16[2,64,128]{2,1,0:T(8,128)(2,1)S(1)}, u32[]{:S(2)}, u32[]{:S(2)}) collective-permute-start(bf16[2,64,128]{2,1,0:T(8,128)(2,1)S(1)} %gather_fusion.6), channel_id=1, source_target_pairs={{0,8},{8,0},{16,24},{24,16},{32,40},{40,32},{48,56},{56,48},{64,72... | collective-permute-start | bytes 98312 | tf_op jit(solution)/shard_map/ppermute | solution.py:19
  66.2 11.8 %collective-permute-start.11 = (bf16[2,64,128]{2,1,0:T(8,128)(2,1)S(1)}, bf16[2,64,128]{2,1,0:T(8,128)(2,1)S(1)}, u32[]{:S(2)}, u32[]{:S(2)}) collective-permute-start(bf16[2,64,128]{2,1,0:T(8,128)(2,1)S(1)} %gather_fusion.14), channel_id=1, source_target_pairs={{0,64},{64,0},{8,72},{72,8},{16,80},{80,16},{24,88},{88,24},{32,96... | collective-permute-start | bytes 98312 | tf_op jit(solution)/shard_map/ppermute | solution.py:19
  68.3 9.7 %collective-permute-start.10 = (bf16[2,64,128]{2,1,0:T(8,128)(2,1)S(1)}, bf16[2,64,128]{2,1,0:T(8,128)(2,1)S(1)}, u32[]{:S(2)}, u32[]{:S(2)}) collective-permute-start(bf16[2,64,128]{2,1,0:T(8,128)(2,1)S(1)} %gather_fusion.13), channel_id=1, source_target_pairs={{0,32},{32,0},{8,40},{40,8},{16,48},{48,16},{24,56},{56,24},{64,96... | collective-permute-start | bytes 98312 | tf_op jit(solution)/shard_map/ppermute | solution.py:19
  70.7 7.3 %collective-permute-start.9 = (bf16[2,64,128]{2,1,0:T(8,128)(2,1)S(1)}, bf16[2,64,128]{2,1,0:T(8,128)(2,1)S(1)}, u32[]{:S(2)}, u32[]{:S(2)}) collective-permute-start(bf16[2,64,128]{2,1,0:T(8,128)(2,1)S(1)} %gather_fusion.12), channel_id=1, source_target_pairs={{0,16},{16,0},{8,24},{24,8},{32,48},{48,32},{40,56},{56,40},{64,80... | collective-permute-start | bytes 98312 | tf_op jit(solution)/shard_map/ppermute | solution.py:19
  73.1 4.9 %collective-permute-start.8 = (bf16[2,64,128]{2,1,0:T(8,128)(2,1)S(1)}, bf16[2,64,128]{2,1,0:T(8,128)(2,1)S(1)}, u32[]{:S(2)}, u32[]{:S(2)}) collective-permute-start(bf16[2,64,128]{2,1,0:T(8,128)(2,1)S(1)} %gather_fusion.11), channel_id=1, source_target_pairs={{0,8},{8,0},{16,24},{24,16},{32,40},{40,32},{48,56},{56,48},{64,72... | collective-permute-start | bytes 98312 | tf_op jit(solution)/shard_map/ppermute | solution.py:19
  85.7 19.0 %collective-permute-start.15 = (bf16[2,64,128]{2,1,0:T(8,128)(2,1)S(1)}, bf16[2,64,128]{2,1,0:T(8,128)(2,1)S(1)}, u32[]{:S(2)}, u32[]{:S(2)}) collective-permute-start(bf16[2,64,128]{2,1,0:T(8,128)(2,1)S(1)} %gather_fusion.19), channel_id=1, source_target_pairs={{0,64},{64,0},{8,72},{72,8},{16,80},{80,16},{24,88},{88,24},{32,96... | collective-permute-start | bytes 98312 | tf_op jit(solution)/shard_map/ppermute | solution.py:19
  91.5 13.1 %collective-permute-start.14 = (bf16[2,64,128]{2,1,0:T(8,128)(2,1)S(1)}, bf16[2,64,128]{2,1,0:T(8,128)(2,1)S(1)}, u32[]{:S(2)}, u32[]{:S(2)}) collective-permute-start(bf16[2,64,128]{2,1,0:T(8,128)(2,1)S(1)} %gather_fusion.18), channel_id=1, source_target_pairs={{0,32},{32,0},{8,40},{40,8},{16,48},{48,16},{24,56},{56,24},{64,96... | collective-permute-start | bytes 98312 | tf_op jit(solution)/shard_map/ppermute | solution.py:19
  95.9 8.8 %collective-permute-start.13 = (bf16[2,64,128]{2,1,0:T(8,128)(2,1)S(1)}, bf16[2,64,128]{2,1,0:T(8,128)(2,1)S(1)}, u32[]{:S(2)}, u32[]{:S(2)}) collective-permute-start(bf16[2,64,128]{2,1,0:T(8,128)(2,1)S(1)} %gather_fusion.17), channel_id=1, source_target_pairs={{0,16},{16,0},{8,24},{24,8},{32,48},{48,32},{40,56},{56,40},{64,80... | collective-permute-start | bytes 98312 | tf_op jit(solution)/shard_map/ppermute | solution.py:19
  99.5 5.1 %collective-permute-start.12 = (bf16[2,64,128]{2,1,0:T(8,128)(2,1)S(1)}, bf16[2,64,128]{2,1,0:T(8,128)(2,1)S(1)}, u32[]{:S(2)}, u32[]{:S(2)}) collective-permute-start(bf16[2,64,128]{2,1,0:T(8,128)(2,1)S(1)} %gather_fusion.16), channel_id=1, source_target_pairs={{0,8},{8,0},{16,24},{24,16},{32,40},{40,32},{48,56},{56,48},{64,72... | collective-permute-start | bytes 98312 | tf_op jit(solution)/shard_map/ppermute | solution.py:19
  109.1 14.9 %copy-start.1 = (bf16[32,64,128]{2,1,0:T(8,128)(2,1)}, bf16[32,64,128]{2,1,0:T(8,128)(2,1)S(1)}, u32[]{:S(2)}) copy-start(bf16[32,64,128]{2,1,0:T(8,128)(2,1)S(1)} %fusion.26) | copy-start | bytes 1572868
  111.3 11.8 %collective-permute-start.19 = (bf16[2,64,128]{2,1,0:T(8,128)(2,1)S(1)}, bf16[2,64,128]{2,1,0:T(8,128)(2,1)S(1)}, u32[]{:S(2)}, u32[]{:S(2)}) collective-permute-start(bf16[2,64,128]{2,1,0:T(8,128)(2,1)S(1)} %gather_fusion.24), channel_id=1, source_target_pairs={{0,64},{64,0},{8,72},{72,8},{16,80},{80,16},{24,88},{88,24},{32,96... | collective-permute-start | bytes 98312 | tf_op jit(solution)/shard_map/ppermute | solution.py:19
  113.4 9.7 %collective-permute-start.18 = (bf16[2,64,128]{2,1,0:T(8,128)(2,1)S(1)}, bf16[2,64,128]{2,1,0:T(8,128)(2,1)S(1)}, u32[]{:S(2)}, u32[]{:S(2)}) collective-permute-start(bf16[2,64,128]{2,1,0:T(8,128)(2,1)S(1)} %gather_fusion.23), channel_id=1, source_target_pairs={{0,32},{32,0},{8,40},{40,8},{16,48},{48,16},{24,56},{56,24},{64,96... | collective-permute-start | bytes 98312 | tf_op jit(solution)/shard_map/ppermute | solution.py:19
  115.8 7.2 %collective-permute-start.17 = (bf16[2,64,128]{2,1,0:T(8,128)(2,1)S(1)}, bf16[2,64,128]{2,1,0:T(8,128)(2,1)S(1)}, u32[]{:S(2)}, u32[]{:S(2)}) collective-permute-start(bf16[2,64,128]{2,1,0:T(8,128)(2,1)S(1)} %gather_fusion.22), channel_id=1, source_target_pairs={{0,16},{16,0},{8,24},{24,8},{32,48},{48,32},{40,56},{56,40},{64,80... | collective-permute-start | bytes 98312 | tf_op jit(solution)/shard_map/ppermute | solution.py:19
  118.2 4.9 %collective-permute-start.16 = (bf16[2,64,128]{2,1,0:T(8,128)(2,1)S(1)}, bf16[2,64,128]{2,1,0:T(8,128)(2,1)S(1)}, u32[]{:S(2)}, u32[]{:S(2)}) collective-permute-start(bf16[2,64,128]{2,1,0:T(8,128)(2,1)S(1)} %gather_fusion.21), channel_id=1, source_target_pairs={{0,8},{8,0},{16,24},{24,16},{32,40},{40,32},{48,56},{56,48},{64,72... | collective-permute-start | bytes 98312 | tf_op jit(solution)/shard_map/ppermute | solution.py:19
  124.0 4.0 %copy-start.7 = (s32[32,64]{1,0:T(8,128)S(1)}, s32[32,64]{1,0:T(8,128)}, u32[]{:S(2)}) copy-start(s32[32,64]{1,0:T(8,128)} %param.33) | copy-start | bytes 24580
  124.0 4.0 %copy-start.9 = (f32[8]{0:T(128)S(1)}, f32[8]{0:T(128)}, u32[]{:S(2)}) copy-start(f32[8]{0:T(128)} %param.34) | copy-start | bytes 100
  124.0 4.2 %copy-start.2 = (bf16[32,64,128]{2,1,0:T(8,128)(2,1)S(1)}, bf16[32,64,128]{2,1,0:T(8,128)(2,1)}, u32[]{:S(2)}) copy-start(bf16[32,64,128]{2,1,0:T(8,128)(2,1)} %param.28) | copy-start | bytes 1572868
  127.9 6.4 %copy-start.8 = (s32[32,3]{0,1:T(4,128)S(1)}, s32[32,3]{0,1:T(4,128)}, u32[]{:S(2)}) copy-start(s32[32,3]{0,1:T(4,128)} %param.31) | copy-start | bytes 1156
  127.9 6.6 %copy-start.5 = (f32[32,64]{1,0:T(8,128)S(1)}, f32[32,64]{1,0:T(8,128)}, u32[]{:S(2)}) copy-start(f32[32,64]{1,0:T(8,128)} %param.29) | copy-start | bytes 24580
  128.7 32.9 %collective-permute-start.20 = (bf16[2,64,128]{2,0,1:T(2,128)(2,1)S(1)}, bf16[2,64,128]{2,0,1:T(2,128)(2,1)S(1)}, u32[]{:S(2)}, u32[]{:S(2)}) collective-permute-start(bf16[2,64,128]{2,0,1:T(2,128)(2,1)S(1)} %get-tuple-element.41), channel_id=1, source_target_pairs={{0,1},{1,2},{2,3},{3,4},{4,5},{5,6},{6,7},{8,9},{9,10},{10,11},{11... | collective-permute-start | bytes 98312 | tf_op jit(solution)/shard_map/ppermute | solution.py:29
  132.7 5.8 %copy-start.11 = (s32[32]{0:T(128)S(1)}, s32[32]{0:T(128)}, u32[]{:S(2)}) copy-start(s32[32]{0:T(128)} %param.27) | copy-start | bytes 388
  132.8 6.0 %copy-start.12 = (s32[32,1]{0,1:T(1,128)S(1)}, s32[32,1]{0,1:T(1,128)}, u32[]{:S(2)}) copy-start(s32[32,1]{0,1:T(1,128)} %param.26) | copy-start | bytes 388
  132.8 29.0 %collective-permute-start.21 = (bf16[2,64,128]{2,0,1:T(2,128)(2,1)S(1)}, bf16[2,64,128]{2,0,1:T(2,128)(2,1)S(1)}, u32[]{:S(2)}, u32[]{:S(2)}) collective-permute-start(bf16[2,64,128]{2,0,1:T(2,128)(2,1)S(1)} %get-tuple-element.40), channel_id=1, source_target_pairs={{1,0},{2,1},{3,2},{4,3},{5,4},{6,5},{7,6},{9,8},{10,9},{11,10},{12... | collective-permute-start | bytes 98312 | tf_op jit(solution)/shard_map/ppermute | solution.py:30
  158.4 3.2 %copy-start.6 = (f32[32,64]{1,0:T(8,128)S(1)}, f32[32,64]{1,0:T(8,128)}, u32[]{:S(2)}) copy-start(f32[32,64]{1,0:T(8,128)} %param.35) | copy-start | bytes 24580
  158.4 3.2 %copy-start.4 = (bf16[4,64,64]{2,1,0:T(8,128)(2,1)S(1)}, bf16[4,64,64]{2,1,0:T(8,128)(2,1)}, u32[]{:S(2)}) copy-start(bf16[4,64,64]{2,1,0:T(8,128)(2,1)} %param.32) | copy-start | bytes 98308
Sparse Core Ops, SparseCore 0:
  128.1 59.6 all-gather.2
where the time goes:
time: 202 us; the launch traced here: 201 us
  starting transfers between devices  74.3 us (37%)
  matrix products  33 us (16%)
  local copies, waits for them, and re-layouts  30 us (15%)
  waiting for transfers between devices  22.6 us (11%)
  blocking collectives  16.9 us (8%)
  between operations  15.3 us (8%)
  other arithmetic  9.17 us (5%)
    ppermute x20, starting transfers between devices, from_partner(): return lax.ppermute(block, axis, route)  68.9 us
    dot_general x6, matrix products, near_product(): jnp.einsum('rkab,rkbc->rac', near_blocks, picked, preferred_element_type=...  23.3 us
    all_gather x1, waiting for transfers between devices, body(): heat_piece = lax.all_gather(heat_b, 'therm', axis=0, tiled=True)  22.6 us
    unnamed x1, blocking collectives  16.9 us
    gather x6, local copies, waits for them, and re-layouts, near_product(): picked = field_b[near_index]  12.8 us
    gather x20, local copies, waits for them, and re-layouts, electric_apply(): outgoing = field_b[interface_tiles_per_level[level_bit]]  11.2 us
    dot_general x1, matrix products, body(): jnp.einsum('jr,rbc->jbc', selector, heat_piece, preferred_element_type=jn...  5.19 us
    unnamed x35, local copies, waits for them, and re-layouts  4.18 us
  transfers between devices with their start and end apart: 23, of which 1 were waited for; matrix products, arithmetic and copies ran while one was open for 14% of the time, Pallas kernels for 0%

commit v1 on v0

--- a/solution.py
+++ b/solution.py
@@ -1,3 +1,4 @@
+import functools
 import jax
 import jax.numpy as jnp
 from jax import lax
@@ -7,6 +8,34 @@
 ZB = 2
 relax_factor = 0.8
 time_increment = 0.5
+
+
+def report_vector_here(inputs, in_dim):
+    top = lax.axis_index("therm")
+    current_arr = lax.axis_size("therm")
+    extra, fresh, item_now = (current_arr, top, inputs.shape[in_dim])
+    blocks_here = [i0 * extra if no == in_dim else i0 for no, i0 in enumerate(inputs.shape)]
+    ready = jnp.zeros(blocks_here, inputs.dtype)
+    f_now = latest = inputs
+    v_now = lax.dynamic_update_slice_in_dim(ready, inputs, fresh * item_now, axis=in_dim)
+    for m in tuple(range(1, extra // 2 + 1)):
+        f_now = lax.ppermute(
+            f_now, axis_name="therm", perm=[(no, (no + 1) % extra) for no in range(extra)]
+        )
+        v_now = lax.dynamic_update_slice_in_dim(
+            v_now, f_now, (fresh - m) % extra * item_now, axis=in_dim
+        )
+        if 2 * m < extra:
+            latest = lax.ppermute(
+                latest, axis_name="therm", perm=[(no, (no - 1) % extra) for no in range(extra)]
+            )
+            v_now = lax.dynamic_update_slice_in_dim(
+                v_now, latest, (fresh + m) % extra * item_now, axis=in_dim
+            )
+    return v_now
+
+
+unite_the_joints = functools.partial(report_vector_here, in_dim=0)
 
 
 def from_partner(block, axis, bit):
@@ -111,7 +140,7 @@
     warmth_tile_count = warmth_values.shape[0]
     block_ids = jnp.arange(warmth_tile_count)[:, None]
     own_index = lax.axis_index("therm")
-    heat_piece = lax.all_gather(heat_b, "therm", axis=0, tiled=True)
+    heat_piece = unite_the_joints(heat_b)
     owner_piece = lax.all_gather(owners, "therm", axis=0, tiled=True)
     row_piece = lax.all_gather(warmth_receiver_tile, "therm", axis=0, tiled=True)
     selector = ((row_piece[None, :] == block_ids) & (owner_piece[None, :] == own_index)).astype(

time: 202 us -> 217 us (1.074)
  the two profiles are of different devices: /device:TPU:1 before, /device:TPU:6 now
where the time goes in v1:
time: 217 us; the launch traced here: 215 us
  starting transfers between devices  93.3 us (43%)
  local copies, waits for them, and re-layouts  35.3 us (16%)
  matrix products  31.5 us (15%)
  waiting for transfers between devices  23.9 us (11%)
  blocking collectives  18 us (8%)
  other arithmetic  11 us (5%)
  between operations  2.33 us (1%)
    ppermute x20, starting transfers between devices, from_partner(): return lax.ppermute(block, axis, route)  64.8 us
    dot_general x6, matrix products, near_product(): jnp.einsum('rkab,rkbc->rac', near_blocks, picked, preferred_element_type=...  23.6 us
    ppermute x4, waiting for transfers between devices, report_vector_here(): lax.ppermute(f_now, axis_name='therm', perm=[(no, (no + 1) % extra) for n...  20.1 us
    unnamed x1, blocking collectives  18 us
    gather x6, local copies, waits for them, and re-layouts, near_product(): picked = field_b[near_index]  12.8 us
    ppermute x4, starting transfers between devices, report_vector_here(): lax.ppermute(f_now, axis_name='therm', perm=[(no, (no + 1) % extra) for n...  11.6 us
    ppermute x3, starting transfers between devices, report_vector_here(): lax.ppermute(latest, axis_name='therm', perm=[(no, (no - 1) % extra) for...  11.3 us
    gather x20, local copies, waits for them, and re-layouts, electric_apply(): outgoing = field_b[interface_tiles_per_level[level_bit]]  11.2 us
  transfers between devices with their start and end apart: 29, of which 6 were waited for; matrix products, arithmetic and copies ran while one was open for 33% of the time, Pallas kernels for 0%

profile of v1, /device:TPU:6, one launch (start us, length us, event | category | flops | bytes accessed | tf_op | source)
XLA Modules:
  0.0 215.3 jit_solution(5975762769222326754)
XLA Ops:
  3.7 1.9 collective-permute-start
  6.2 3.5 %collective-permute-start.1 = (bf16[2,64,128]{2,1,0:T(8,128)(2,1)S(1)}, bf16[2,64,128]{2,1,0:T(8,128)(2,1)S(1)}, u32[]{:S(2)}, u32[]{:S(2)}) collective-permute-start(bf16[2,64,128]{2,1,0:T(8,128)(2,1)S(1)} %gather_fusion.2), channel_id=1, source_target_pairs={{0,16},{16,0},{8,24},{24,8},{32,48},{48,32},{40,56},{56,40},{64,80... | collective-permute-start | bytes 98312 | tf_op jit(solution)/shard_map/ppermute | solution.py:48
  10.3 4.5 %collective-permute-start.2 = (bf16[2,64,128]{2,1,0:T(8,128)(2,1)S(1)}, bf16[2,64,128]{2,1,0:T(8,128)(2,1)}, u32[]{:S(2)}, u32[]{:S(2)}) collective-permute-start(bf16[2,64,128]{2,1,0:T(8,128)(2,1)S(1)} %gather_fusion.3), channel_id=1, source_target_pairs={{0,32},{32,0},{8,40},{40,8},{16,48},{48,16},{24,56},{56,24},{64,96... | collective-permute-start | bytes 98312 | tf_op jit(solution)/shard_map/ppermute | solution.py:48
  15.4 5.0 %collective-permute-start.3 = (bf16[2,64,128]{2,1,0:T(8,128)(2,1)S(1)}, bf16[2,64,128]{2,1,0:T(8,128)(2,1)}, u32[]{:S(2)}, u32[]{:S(2)}) collective-permute-start(bf16[2,64,128]{2,1,0:T(8,128)(2,1)S(1)} %gather_fusion.4), channel_id=1, source_target_pairs={{0,64},{64,0},{8,72},{72,8},{16,80},{80,16},{24,88},{88,24},{32,96... | collective-permute-start | bytes 98312 | tf_op jit(solution)/shard_map/ppermute | solution.py:48
  23.8 4.3 %collective-permute-start.27 = (bf16[2,64,128]{2,0,1:T(2,128)(2,1)S(1)}, bf16[2,64,128]{2,0,1:T(2,128)(2,1)S(1)}, u32[]{:S(2)}, u32[]{:S(2)}) collective-permute-start(bf16[2,64,128]{2,0,1:T(2,128)(2,1)S(1)} %get-tuple-element.39), channel_id=1, source_target_pairs={{0,1},{1,2},{2,3},{3,4},{4,5},{5,6},{6,7},{8,9},{9,10},{10,11},{11... | collective-permute-start | bytes 98312 | tf_op jit(solution)/shard_map/ppermute | solution.py:58
  28.5 2.2 %gather_fusion = bf16[128,64,128]{2,1,0:T(8,128)(2,1)} fusion(bf16[32,64,128]{2,1,0:T(8,128)(2,1)S(1)} %fusion.32, s32[1024]{0:T(1024)S(1)} %pad_clamp_fusion.5), kind=kCustom, calls=%fused_computation | custom fusion | bytes 4194816 | tf_op jit(solution)/shard_map/gather | solution.py:65
  32.7 4.1 %fusion.112 = (bf16[32,64,128]{2,1,0:T(8,128)(2,1)S(1)}, f32[32,64,128]{2,1,0:T(8,128)}) fusion(f32[32,64,128]{2,0,1:T(8,128)S(1)} %fusion.41, bf16[32,4,64,64]{3,2,1,0:T(8,128)(2,1)S(1)} %copy-done, bf16[32,4,64,128]{3,2,1,0:T(8,128)(2,1)} %bitcast.202, f32[32,64]{1,0:T(8,128)S(1)} %copy-done.8, bf16[32,64,128]{2,1,0:T(8,128)(2,1)S(1)} %copy-done.7), kind=kOutput, calls=%fused_computation.191 | convolution fusion | flops 137625600 | bytes 6299648 | tf_op jit(solution)/shard_map/rkab,rkbc->rac/dot_general | solution.py:66
  39.1 1.9 collective-permute-start.4
  41.0 3.3 %collective-permute-start.5 = (bf16[2,64,128]{2,1,0:T(8,128)(2,1)S(1)}, bf16[2,64,128]{2,1,0:T(8,128)(2,1)S(1)}, u32[]{:S(2)}, u32[]{:S(2)}) collective-permute-start(bf16[2,64,128]{2,1,0:T(8,128)(2,1)S(1)} %gather_fusion.7), channel_id=1, source_target_pairs={{0,16},{16,0},{8,24},{24,8},{32,48},{48,32},{40,56},{56,40},{64,80... | collective-permute-start | bytes 98312 | tf_op jit(solution)/shard_map/ppermute | solution.py:48
  44.3 4.0 %collective-permute-start.6 = (bf16[2,64,128]{2,1,0:T(8,128)(2,1)S(1)}, bf16[2,64,128]{2,1,0:T(8,128)(2,1)}, u32[]{:S(2)}, u32[]{:S(2)}) collective-permute-start(bf16[2,64,128]{2,1,0:T(8,128)(2,1)S(1)} %gather_fusion.8), channel_id=1, source_target_pairs={{0,32},{32,0},{8,40},{40,8},{16,48},{48,16},{24,56},{56,24},{64,96... | collective-permute-start | bytes 98312 | tf_op jit(solution)/shard_map/ppermute | solution.py:48
  48.3 2.0 collective-permute-start.7
  51.6 1.9 gather_fusion.25
  53.6 2.2 %gather_fusion.5 = bf16[128,64,128]{2,1,0:T(8,128)(2,1)} fusion(bf16[32,64,128]{2,1,0:T(8,128)(2,1)S(1)} %get-tuple-element.40, s32[1024]{0:T(1024)S(1)} %pad_clamp_fusion.5), kind=kCustom, calls=%fused_computation.5 | custom fusion | bytes 4194816 | tf_op jit(solution)/shard_map/gather | solution.py:65
  55.8 2.7 %collective-permute-done.7 = bf16[2,64,128]{2,1,0:T(8,128)(2,1)} collective-permute-done((bf16[2,64,128]{2,1,0:T(8,128)(2,1)S(1)}, bf16[2,64,128]{2,1,0:T(8,128)(2,1)}, u32[]{:S(2)}, u32[]{:S(2)}) %collective-permute-start.7) | collective-permute-done | bytes 32800 | tf_op jit(solution)/shard_map/ppermute | solution.py:48
  60.1 4.5 %fusion.113 = (bf16[32,64,128]{2,1,0:T(8,128)(2,1)S(1)}, f32[32,64,128]{2,1,0:T(8,128)}) fusion(f32[32,64,128]{2,1,0:T(8,128)} %get-tuple-element.41, f32[32,64,128]{2,0,1:T(8,128)S(1)} %fusion.39, bf16[32,4,64,64]{3,2,1,0:T(8,128)(2,1)S(1)} %copy-done, bf16[32,4,64,128]{3,2,1,0:T(8,128)(2,1)} %bitcast.203, ...), kind=kOutput, calls=%fused_computation.192 | convolution fusion | flops 136839168 | bytes 7872512 | tf_op jit(solution)/shard_map/rkab,rkbc->rac/dot_general | solution.py:66
  66.8 2.4 %collective-permute-start.10 = (bf16[2,64,128]{2,1,0:T(8,128)(2,1)S(1)}, bf16[2,64,128]{2,1,0:T(8,128)(2,1)S(1)}, u32[]{:S(2)}, u32[]{:S(2)}) collective-permute-start(bf16[2,64,128]{2,1,0:T(8,128)(2,1)S(1)} %gather_fusion.13), channel_id=1, source_target_pairs={{0,32},{32,0},{8,40},{40,8},{16,48},{48,16},{24,56},{56,24},{64,96... | collective-permute-start | bytes 98312 | tf_op jit(solution)/shard_map/ppermute | solution.py:48
  69.3 1.9 collective-permute-start.8
  71.2 2.9 %collective-permute-start.9 = (bf16[2,64,128]{2,1,0:T(8,128)(2,1)S(1)}, bf16[2,64,128]{2,1,0:T(8,128)(2,1)S(1)}, u32[]{:S(2)}, u32[]{:S(2)}) collective-permute-start(bf16[2,64,128]{2,1,0:T(8,128)(2,1)S(1)} %gather_fusion.12), channel_id=1, source_target_pairs={{0,16},{16,0},{8,24},{24,8},{32,48},{48,32},{40,56},{56,40},{64,80... | collective-permute-start | bytes 98312 | tf_op jit(solution)/shard_map/ppermute | solution.py:48
  74.2 5.0 %collective-permute-start.11 = (bf16[2,64,128]{2,1,0:T(8,128)(2,1)S(1)}, bf16[2,64,128]{2,1,0:T(8,128)(2,1)S(1)}, u32[]{:S(2)}, u32[]{:S(2)}) collective-permute-start(bf16[2,64,128]{2,1,0:T(8,128)(2,1)S(1)} %gather_fusion.14), channel_id=1, source_target_pairs={{0,64},{64,0},{8,72},{72,8},{16,80},{80,16},{24,88},{88,24},{32,96... | collective-permute-start | bytes 98312 | tf_op jit(solution)/shard_map/ppermute | solution.py:48
  79.2 3.6 %convolution_bitcast_fusion = f32[32,128,64]{1,2,0:T(8,128)} fusion(bf16[32,3,64,64]{3,2,1,0:T(8,128)(2,1)} %param.30, bf16[32,3,64,128]{3,2,1,0:T(8,128)(2,1)} %bitcast.201), kind=kOutput, calls=%fused_computation.34 | convolution fusion | flops 100663296 | bytes 3407872 | tf_op jit(solution)/shard_map/rkab,rkbc->rac/dot_general | solution.py:66
  82.9 2.2 %gather_fusion.10 = bf16[128,64,128]{2,1,0:T(8,128)(2,1)} fusion(bf16[32,64,128]{2,1,0:T(8,128)(2,1)S(1)} %get-tuple-element.42, s32[1024]{0:T(1024)S(1)} %pad_clamp_fusion.5), kind=kCustom, calls=%fused_computation.10 | custom fusion | bytes 4194816 | tf_op jit(solution)/shard_map/gather | solution.py:65
  85.9 4.7 %fusion.114 = (bf16[32,64,128]{2,1,0:T(8,128)(2,1)S(1)}, f32[32,64,128]{2,1,0:T(8,128)}) fusion(f32[32,64,128]{2,1,0:T(8,128)} %get-tuple-element.43, f32[32,64,128]{2,0,1:T(8,128)S(1)} %fusion.37, bf16[32,4,64,64]{3,2,1,0:T(8,128)(2,1)S(1)} %copy-done, bf16[32,4,64,128]{3,2,1,0:T(8,128)(2,1)} %bitcast.204, bf16[32,64,128]{2,1,0:T(8,128)(2,1)} %copy-done.2, ...), kind=kOutput, calls=%fused_computation.193 | convolution fusion | flops 136839168 | bytes 7872512 | tf_op jit(solution)/shard_map/rkab,rkbc->rac/dot_general | solution.py:66
  92.9 1.9 collective-permute-start.12
  94.8 3.2 %collective-permute-start.13 = (bf16[2,64,128]{2,1,0:T(8,128)(2,1)S(1)}, bf16[2,64,128]{2,1,0:T(8,128)(2,1)S(1)}, u32[]{:S(2)}, u32[]{:S(2)}) collective-permute-start(bf16[2,64,128]{2,1,0:T(8,128)(2,1)S(1)} %gather_fusion.17), channel_id=1, source_target_pairs={{0,16},{16,0},{8,24},{24,8},{32,48},{48,32},{40,56},{56,40},{64,80... | collective-permute-start | bytes 98312 | tf_op jit(solution)/shard_map/ppermute | solution.py:48
  98.1 4.1 %collective-permute-start.14 = (bf16[2,64,128]{2,1,0:T(8,128)(2,1)S(1)}, bf16[2,64,128]{2,1,0:T(8,128)(2,1)}, u32[]{:S(2)}, u32[]{:S(2)}) collective-permute-start(bf16[2,64,128]{2,1,0:T(8,128)(2,1)S(1)} %gather_fusion.18), channel_id=1, source_target_pairs={{0,32},{32,0},{8,40},{40,8},{16,48},{48,16},{24,56},{56,24},{64,96... | collective-permute-start | bytes 98312 | tf_op jit(solution)/shard_map/ppermute | solution.py:48
  102.2 4.8 %collective-permute-start.15 = (bf16[2,64,128]{2,1,0:T(8,128)(2,1)S(1)}, bf16[2,64,128]{2,1,0:T(8,128)(2,1)}, u32[]{:S(2)}, u32[]{:S(2)}) collective-permute-start(bf16[2,64,128]{2,1,0:T(8,128)(2,1)S(1)} %gather_fusion.19), channel_id=1, source_target_pairs={{0,64},{64,0},{8,72},{72,8},{16,80},{80,16},{24,88},{88,24},{32,96... | collective-permute-start | bytes 98312 | tf_op jit(solution)/shard_map/ppermute | solution.py:48
  107.0 3.9 %bitcast_add_fusion = f32[32,64,128]{2,0,1:T(8,128)} fusion(f32[32,128,64]{1,2,0:T(8,128)} %convolution_bitcast_fusion, f32[32,64]{0,1:T(8,128)S(1)} %copy.86, bf16[32,64,128]{2,1,0:T(8,128)(2,1)S(1)} %copy-done.4, f32[32,64]{0,1:T(8,128)S(1)} %copy.87), kind=kLoop, calls=%fused_computation.79 | loop fusion | flops 2359296 | bytes 2637824 | tf_op jit(solution)/shard_map/add | solution.py:162
  112.8 2.2 %gather_fusion.15 = bf16[128,64,128]{2,1,0:T(8,128)(2,1)} fusion(bf16[32,64,128]{2,1,0:T(8,128)(2,1)S(1)} %get-tuple-element.44, s32[1024]{0:T(1024)S(1)} %pad_clamp_fusion.5), kind=kCustom, calls=%fused_computation.15 | custom fusion | bytes 4194816 | tf_op jit(solution)/shard_map/gather | solution.py:65
  116.7 3.6 %fusion.20 = bf16[32,64,128]{2,1,0:T(8,128)(2,1)S(1)} fusion(f32[32,64,128]{2,1,0:T(8,128)} %get-tuple-element.45, bf16[32,4,64,64]{3,2,1,0:T(8,128)(2,1)S(1)} %copy-done, bf16[32,4,64,128]{3,2,1,0:T(8,128)(2,1)} %bitcast.205, bf16[32,64,128]{2,1,0:T(8,128)(2,1)} %param.20, f32[32,64,128]{2,0,1:T(8,128)S(1)} %fusion.35, ...), kind=kOutput, calls=%fused_computation.62 | convolution fusion | flops 136839168 | bytes 6823936 | tf_op jit(solution)/shard_map/rkab,rkbc->rac/dot_general | solution.py:66
  122.5 1.9 collective-permute-start.16
  124.4 2.7 %collective-permute-start.17 = (bf16[2,64,128]{2,1,0:T(8,128)(2,1)S(1)}, bf16[2,64,128]{2,1,0:T(8,128)(2,1)S(1)}, u32[]{:S(2)}, u32[]{:S(2)}) collective-permute-start(bf16[2,64,128]{2,1,0:T(8,128)(2,1)S(1)} %gather_fusion.22), channel_id=1, source_target_pairs={{0,16},{16,0},{8,24},{24,8},{32,48},{48,32},{40,56},{56,40},{64,80... | collective-permute-start | bytes 98312 | tf_op jit(solution)/shard_map/ppermute | solution.py:48
  127.1 2.7 %collective-permute-start.18 = (bf16[2,64,128]{2,1,0:T(8,128)(2,1)S(1)}, bf16[2,64,128]{2,1,0:T(8,128)(2,1)S(1)}, u32[]{:S(2)}, u32[]{:S(2)}) collective-permute-start(bf16[2,64,128]{2,1,0:T(8,128)(2,1)S(1)} %gather_fusion.23), channel_id=1, source_target_pairs={{0,32},{32,0},{8,40},{40,8},{16,48},{48,16},{24,56},{56,24},{64,96... | collective-permute-start | bytes 98312 | tf_op jit(solution)/shard_map/ppermute | solution.py:48
  129.8 5.0 %collective-permute-start.19 = (bf16[2,64,128]{2,1,0:T(8,128)(2,1)S(1)}, bf16[2,64,128]{2,1,0:T(8,128)(2,1)S(1)}, u32[]{:S(2)}, u32[]{:S(2)}) collective-permute-start(bf16[2,64,128]{2,1,0:T(8,128)(2,1)S(1)} %gather_fusion.24), channel_id=1, source_target_pairs={{0,64},{64,0},{8,72},{72,8},{16,80},{80,16},{24,88},{88,24},{32,96... | collective-permute-start | bytes 98312 | tf_op jit(solution)/shard_map/ppermute | solution.py:48
  135.2 18.0 %all-reduce.2 = (s32[256]{0:T(256)S(1)}, s32[256]{0:T(256)S(1)}) all-reduce(s32[256]{0:T(256)S(1)} %dynamic-update-slice.6, s32[256]{0:T(256)S(1)} %bitcast_dynamic-update-slice_fusion), channel_id=1, replica_groups=mesh['elec'=64,'therm'=8] {'therm'}, use_global_device_ids=true, to_apply=%add | all-reduce | flops 512 | bytes 4096
  153.2 2.2 %gather_fusion.20 = bf16[128,64,128]{2,1,0:T(8,128)(2,1)} fusion(bf16[32,64,128]{2,1,0:T(8,128)(2,1)S(1)} %fusion.20, s32[1024]{0:T(1024)S(1)} %pad_clamp_fusion.5), kind=kCustom, calls=%fused_computation.20 | custom fusion | bytes 4194816 | tf_op jit(solution)/shard_map/gather | solution.py:65
  157.6 3.1 %fusion.17 = bf16[32,64,128]{2,1,0:T(8,128)(2,1)S(1)} fusion(bf16[32,4,64,64]{3,2,1,0:T(8,128)(2,1)S(1)} %copy-done, bf16[32,4,64,128]{3,2,1,0:T(8,128)(2,1)} %bitcast.200, bf16[32,64,128]{2,1,0:T(8,128)(2,1)S(1)} %fusion.20, f32[32,64,128]{2,0,1:T(8,128)S(1)} %fusion.33, f32[32,64]{1,0:T(8,128)S(1)} %copy-done.8), kind=kOutput, calls=%fused_computation.59 | convolution fusion | flops 135790592 | bytes 5251072 | tf_op jit(solution)/shard_map/rkab,rkbc->rac/dot_general | solution.py:66
  160.6 4.6 %collective-permute-start.20 = (bf16[32,64,128]{2,1,0:T(8,128)(2,1)S(1)}, bf16[32,64,128]{2,1,0:T(8,128)(2,1)S(1)}, u32[]{:S(2)}, u32[]{:S(2)}) collective-permute-start(bf16[32,64,128]{2,1,0:T(8,128)(2,1)S(1)} %fusion.17), channel_id=1, source_target_pairs={{0,1},{1,2},{2,3},{3,4},{4,5},{5,6},{6,7},{7,0},{8,9},{9,10},{10,1... | collective-permute-start | bytes 1572872 | tf_op jit(solution)/shard_map/ppermute | solution.py:22
  165.5 2.5 %collective-permute-start.21 = (bf16[32,64,128]{2,1,0:T(8,128)(2,1)S(1)}, bf16[32,64,128]{2,1,0:T(8,128)(2,1)S(1)}, u32[]{:S(2)}, u32[]{:S(2)}) collective-permute-start(bf16[32,64,128]{2,1,0:T(8,128)(2,1)S(1)} %fusion.17), channel_id=1, source_target_pairs={{0,7},{1,0},{2,1},{3,2},{4,3},{5,4},{6,5},{7,6},{8,15},{9,8},{10,9... | collective-permute-start | bytes 1572872 | tf_op jit(solution)/shard_map/ppermute | solution.py:29
  169.7 4.9 %collective-permute-done.20 = bf16[32,64,128]{2,1,0:T(8,128)(2,1)S(1)} collective-permute-done((bf16[32,64,128]{2,1,0:T(8,128)(2,1)S(1)}, bf16[32,64,128]{2,1,0:T(8,128)(2,1)S(1)}, u32[]{:S(2)}, u32[]{:S(2)}) %collective-permute-start.20) | collective-permute-done | bytes 524320 | tf_op jit(solution)/shard_map/ppermute | solution.py:22
  174.6 3.1 %collective-permute-start.22 = (bf16[32,64,128]{2,1,0:T(8,128)(2,1)S(1)}, bf16[32,64,128]{2,1,0:T(8,128)(2,1)S(1)}, u32[]{:S(2)}, u32[]{:S(2)}) collective-permute-start(bf16[32,64,128]{2,1,0:T(8,128)(2,1)S(1)} %collective-permute-done.20), channel_id=1, source_target_pairs={{0,1},{1,2},{2,3},{3,4},{4,5},{5,6},{6,7},{7,0},{8,9},{9,10},{10,1... | collective-permute-start | bytes 1572872 | tf_op jit(solution)/shard_map/ppermute | solution.py:22
  177.8 1.7 fusion.78
  179.4 4.0 %collective-permute-start.23 = (bf16[32,64,128]{2,1,0:T(8,128)(2,1)S(1)}, bf16[32,64,128]{2,1,0:T(8,128)(2,1)S(1)}, u32[]{:S(2)}, u32[]{:S(2)}) collective-permute-start(bf16[32,64,128]{2,1,0:T(8,128)(2,1)S(1)} %collective-permute-done.21), channel_id=1, source_target_pairs={{0,7},{1,0},{2,1},{3,2},{4,3},{5,4},{6,5},{7,6},{8,15},{9,8},{10,9... | collective-permute-start | bytes 1572872 | tf_op jit(solution)/shard_map/ppermute | solution.py:29
  184.8 2.8 %collective-permute-done.22 = bf16[32,64,128]{2,1,0:T(8,128)(2,1)S(1)} collective-permute-done((bf16[32,64,128]{2,1,0:T(8,128)(2,1)S(1)}, bf16[32,64,128]{2,1,0:T(8,128)(2,1)S(1)}, u32[]{:S(2)}, u32[]{:S(2)}) %collective-permute-start.22) | collective-permute-done | bytes 524320 | tf_op jit(solution)/shard_map/ppermute | solution.py:22
  187.6 1.9 collective-permute-start.24
  191.4 4.8 %collective-permute-start.25 = (bf16[32,64,128]{2,1,0:T(8,128)(2,1)S(1)}, bf16[32,64,128]{2,1,0:T(8,128)(2,1)S(1)}, u32[]{:S(2)}, u32[]{:S(2)}) collective-permute-start(bf16[32,64,128]{2,1,0:T(8,128)(2,1)S(1)} %collective-permute-done.23), channel_id=1, source_target_pairs={{0,7},{1,0},{2,1},{3,2},{4,3},{5,4},{6,5},{7,6},{8,15},{9,8},{10,9... | collective-permute-start | bytes 1572872 | tf_op jit(solution)/shard_map/ppermute | solution.py:29
  196.6 3.5 %collective-permute-done.24 = bf16[32,64,128]{2,1,0:T(8,128)(2,1)S(1)} collective-permute-done((bf16[32,64,128]{2,1,0:T(8,128)(2,1)S(1)}, bf16[32,64,128]{2,1,0:T(8,128)(2,1)S(1)}, u32[]{:S(2)}, u32[]{:S(2)}) %collective-permute-start.24) | collective-permute-done | bytes 524320 | tf_op jit(solution)/shard_map/ppermute | solution.py:22
  200.1 2.1 collective-permute-start.26
  203.4 9.0 %collective-permute-done.26 = bf16[32,64,128]{2,1,0:T(8,128)(2,1)S(1)} collective-permute-done((bf16[32,64,128]{2,1,0:T(8,128)(2,1)S(1)}, bf16[32,64,128]{2,1,0:T(8,128)(2,1)S(1)}, u32[]{:S(2)}, u32[]{:S(2)}) %collective-permute-start.26) | collective-permute-done | bytes 524320 | tf_op jit(solution)/shard_map/ppermute | solution.py:22
  (142 shorter events, 38.3 us)
Async XLA Ops:
  0.6 32.1 %copy-start = (bf16[32,4,64,64]{3,2,1,0:T(8,128)(2,1)S(1)}, bf16[32,4,64,64]{3,2,1,0:T(8,128)(2,1)}, u32[]{:S(2)}) copy-start(bf16[32,4,64,64]{3,2,1,0:T(8,128)(2,1)} %param.22) | copy-start | bytes 3145732
  0.6 27.7 %copy-start.10 = (s32[4,2]{0,1:T(2,128)S(1)}, s32[4,2]{0,1:T(2,128)}, u32[]{:S(2)}) copy-start(s32[4,2]{0,1:T(2,128)} %param.24) | copy-start | bytes 100
  0.7 27.4 %copy-start.13 = (s32[32,4]{0,1:T(4,128)S(1)}, s32[32,4]{0,1:T(4,128)}, u32[]{:S(2)}) copy-start(s32[32,4]{0,1:T(4,128)} %param.23) | copy-start | bytes 1540
  0.7 27.6 %copy-start.14 = (s32[32,3]{0,1:T(4,128)S(1)}, s32[32,3]{0,1:T(4,128)}, u32[]{:S(2)}) copy-start(s32[32,3]{0,1:T(4,128)} %param.31) | copy-start | bytes 1156
  3.7 27.1 %collective-permute-start = (bf16[2,64,128]{2,1,0:T(8,128)(2,1)S(1)}, bf16[2,64,128]{2,1,0:T(8,128)(2,1)S(1)}, u32[]{:S(2)}, u32[]{:S(2)}) collective-permute-start(bf16[2,64,128]{2,1,0:T(8,128)(2,1)S(1)} %gather_fusion.1), channel_id=1, source_target_pairs={{0,8},{8,0},{16,24},{24,16},{32,40},{40,32},{48,56},{56,48},{64,72... | collective-permute-start | bytes 98312 | tf_op jit(solution)/shard_map/ppermute | solution.py:48
  6.2 24.7 %collective-permute-start.1 = (bf16[2,64,128]{2,1,0:T(8,128)(2,1)S(1)}, bf16[2,64,128]{2,1,0:T(8,128)(2,1)S(1)}, u32[]{:S(2)}, u32[]{:S(2)}) collective-permute-start(bf16[2,64,128]{2,1,0:T(8,128)(2,1)S(1)} %gather_fusion.2), channel_id=1, source_target_pairs={{0,16},{16,0},{8,24},{24,8},{32,48},{48,32},{40,56},{56,40},{64,80... | collective-permute-start | bytes 98312 | tf_op jit(solution)/shard_map/ppermute | solution.py:48
  10.3 20.6 %collective-permute-start.2 = (bf16[2,64,128]{2,1,0:T(8,128)(2,1)S(1)}, bf16[2,64,128]{2,1,0:T(8,128)(2,1)}, u32[]{:S(2)}, u32[]{:S(2)}) collective-permute-start(bf16[2,64,128]{2,1,0:T(8,128)(2,1)S(1)} %gather_fusion.3), channel_id=1, source_target_pairs={{0,32},{32,0},{8,40},{40,8},{16,48},{48,16},{24,56},{56,24},{64,96... | collective-permute-start | bytes 98312 | tf_op jit(solution)/shard_map/ppermute | solution.py:48
  15.4 15.5 %collective-permute-start.3 = (bf16[2,64,128]{2,1,0:T(8,128)(2,1)S(1)}, bf16[2,64,128]{2,1,0:T(8,128)(2,1)}, u32[]{:S(2)}, u32[]{:S(2)}) collective-permute-start(bf16[2,64,128]{2,1,0:T(8,128)(2,1)S(1)} %gather_fusion.4), channel_id=1, source_target_pairs={{0,64},{64,0},{8,72},{72,8},{16,80},{80,16},{24,88},{88,24},{32,96... | collective-permute-start | bytes 98312 | tf_op jit(solution)/shard_map/ppermute | solution.py:48
  23.8 141.6 %collective-permute-start.27 = (bf16[2,64,128]{2,0,1:T(2,128)(2,1)S(1)}, bf16[2,64,128]{2,0,1:T(2,128)(2,1)S(1)}, u32[]{:S(2)}, u32[]{:S(2)}) collective-permute-start(bf16[2,64,128]{2,0,1:T(2,128)(2,1)S(1)} %get-tuple-element.39), channel_id=1, source_target_pairs={{0,1},{1,2},{2,3},{3,4},{4,5},{5,6},{6,7},{8,9},{9,10},{10,11},{11... | collective-permute-start | bytes 98312 | tf_op jit(solution)/shard_map/ppermute | solution.py:58
  28.5 4.2 %copy-start.7 = (bf16[32,64,128]{2,1,0:T(8,128)(2,1)S(1)}, bf16[32,64,128]{2,1,0:T(8,128)(2,1)}, u32[]{:S(2)}) copy-start(bf16[32,64,128]{2,1,0:T(8,128)(2,1)} %param.20) | copy-start | bytes 1572868
  28.5 4.2 %copy-start.8 = (f32[32,64]{1,0:T(8,128)S(1)}, f32[32,64]{1,0:T(8,128)}, u32[]{:S(2)}) copy-start(f32[32,64]{1,0:T(8,128)} %param.21) | copy-start | bytes 24580
  39.1 16.7 %collective-permute-start.4 = (bf16[2,64,128]{2,1,0:T(8,128)(2,1)S(1)}, bf16[2,64,128]{2,1,0:T(8,128)(2,1)S(1)}, u32[]{:S(2)}, u32[]{:S(2)}) collective-permute-start(bf16[2,64,128]{2,1,0:T(8,128)(2,1)S(1)} %gather_fusion.6), channel_id=1, source_target_pairs={{0,8},{8,0},{16,24},{24,16},{32,40},{40,32},{48,56},{56,48},{64,72... | collective-permute-start | bytes 98312 | tf_op jit(solution)/shard_map/ppermute | solution.py:48
  41.0 14.7 %collective-permute-start.5 = (bf16[2,64,128]{2,1,0:T(8,128)(2,1)S(1)}, bf16[2,64,128]{2,1,0:T(8,128)(2,1)S(1)}, u32[]{:S(2)}, u32[]{:S(2)}) collective-permute-start(bf16[2,64,128]{2,1,0:T(8,128)(2,1)S(1)} %gather_fusion.7), channel_id=1, source_target_pairs={{0,16},{16,0},{8,24},{24,8},{32,48},{48,32},{40,56},{56,40},{64,80... | collective-permute-start | bytes 98312 | tf_op jit(solution)/shard_map/ppermute | solution.py:48
  44.3 11.5 %collective-permute-start.6 = (bf16[2,64,128]{2,1,0:T(8,128)(2,1)S(1)}, bf16[2,64,128]{2,1,0:T(8,128)(2,1)}, u32[]{:S(2)}, u32[]{:S(2)}) collective-permute-start(bf16[2,64,128]{2,1,0:T(8,128)(2,1)S(1)} %gather_fusion.8), channel_id=1, source_target_pairs={{0,32},{32,0},{8,40},{40,8},{16,48},{48,16},{24,56},{56,24},{64,96... | collective-permute-start | bytes 98312 | tf_op jit(solution)/shard_map/ppermute | solution.py:48
  48.3 10.1 %collective-permute-start.7 = (bf16[2,64,128]{2,1,0:T(8,128)(2,1)S(1)}, bf16[2,64,128]{2,1,0:T(8,128)(2,1)}, u32[]{:S(2)}, u32[]{:S(2)}) collective-permute-start(bf16[2,64,128]{2,1,0:T(8,128)(2,1)S(1)} %gather_fusion.9), channel_id=1, source_target_pairs={{0,64},{64,0},{8,72},{72,8},{16,80},{80,16},{24,88},{88,24},{32,96... | collective-permute-start | bytes 98312 | tf_op jit(solution)/shard_map/ppermute | solution.py:48
  53.6 4.8 %copy-start.15 = (bf16[8,64,64]{2,1,0:T(8,128)(2,1)S(1)}, bf16[8,64,64]{2,1,0:T(8,128)(2,1)}, u32[]{:S(2)}) copy-start(bf16[8,64,64]{2,1,0:T(8,128)(2,1)} %param.25) | copy-start | bytes 196612
  64.6 18.3 %copy-start.2 = (bf16[32,64,128]{2,1,0:T(8,128)(2,1)}, bf16[32,64,128]{2,1,0:T(8,128)(2,1)S(1)}, u32[]{:S(2)}) copy-start(bf16[32,64,128]{2,1,0:T(8,128)(2,1)S(1)} %get-tuple-element.42) | copy-start | bytes 1572868
  66.8 18.2 %collective-permute-start.10 = (bf16[2,64,128]{2,1,0:T(8,128)(2,1)S(1)}, bf16[2,64,128]{2,1,0:T(8,128)(2,1)S(1)}, u32[]{:S(2)}, u32[]{:S(2)}) collective-permute-start(bf16[2,64,128]{2,1,0:T(8,128)(2,1)S(1)} %gather_fusion.13), channel_id=1, source_target_pairs={{0,32},{32,0},{8,40},{40,8},{16,48},{48,16},{24,56},{56,24},{64,96... | collective-permute-start | bytes 98312 | tf_op jit(solution)/shard_map/ppermute | solution.py:48
  69.3 15.8 %collective-permute-start.8 = (bf16[2,64,128]{2,1,0:T(8,128)(2,1)S(1)}, bf16[2,64,128]{2,1,0:T(8,128)(2,1)S(1)}, u32[]{:S(2)}, u32[]{:S(2)}) collective-permute-start(bf16[2,64,128]{2,1,0:T(8,128)(2,1)S(1)} %gather_fusion.11), channel_id=1, source_target_pairs={{0,8},{8,0},{16,24},{24,16},{32,40},{40,32},{48,56},{56,48},{64,72... | collective-permute-start | bytes 98312 | tf_op jit(solution)/shard_map/ppermute | solution.py:48
  71.2 13.8 %collective-permute-start.9 = (bf16[2,64,128]{2,1,0:T(8,128)(2,1)S(1)}, bf16[2,64,128]{2,1,0:T(8,128)(2,1)S(1)}, u32[]{:S(2)}, u32[]{:S(2)}) collective-permute-start(bf16[2,64,128]{2,1,0:T(8,128)(2,1)S(1)} %gather_fusion.12), channel_id=1, source_target_pairs={{0,16},{16,0},{8,24},{24,8},{32,48},{48,32},{40,56},{56,40},{64,80... | collective-permute-start | bytes 98312 | tf_op jit(solution)/shard_map/ppermute | solution.py:48
  74.2 10.9 %collective-permute-start.11 = (bf16[2,64,128]{2,1,0:T(8,128)(2,1)S(1)}, bf16[2,64,128]{2,1,0:T(8,128)(2,1)S(1)}, u32[]{:S(2)}, u32[]{:S(2)}) collective-permute-start(bf16[2,64,128]{2,1,0:T(8,128)(2,1)S(1)} %gather_fusion.14), channel_id=1, source_target_pairs={{0,64},{64,0},{8,72},{72,8},{16,80},{80,16},{24,88},{88,24},{32,96... | collective-permute-start | bytes 98312 | tf_op jit(solution)/shard_map/ppermute | solution.py:48
  79.2 3.6 %copy-start.11 = (f32[32,64]{1,0:T(8,128)S(1)}, f32[32,64]{1,0:T(8,128)}, u32[]{:S(2)}) copy-start(f32[32,64]{1,0:T(8,128)} %param.29) | copy-start | bytes 24580
  85.9 21.1 %copy-start.4 = (bf16[32,64,128]{2,1,0:T(8,128)(2,1)S(1)}, bf16[32,64,128]{2,1,0:T(8,128)(2,1)}, u32[]{:S(2)}) copy-start(bf16[32,64,128]{2,1,0:T(8,128)(2,1)} %param.28) | copy-start | bytes 1572868
  92.9 22.1 %collective-permute-start.12 = (bf16[2,64,128]{2,1,0:T(8,128)(2,1)S(1)}, bf16[2,64,128]{2,1,0:T(8,128)(2,1)S(1)}, u32[]{:S(2)}, u32[]{:S(2)}) collective-permute-start(bf16[2,64,128]{2,1,0:T(8,128)(2,1)S(1)} %gather_fusion.16), channel_id=1, source_target_pairs={{0,8},{8,0},{16,24},{24,16},{32,40},{40,32},{48,56},{56,48},{64,72... | collective-permute-start | bytes 98312 | tf_op jit(solution)/shard_map/ppermute | solution.py:48
  94.8 20.1 %collective-permute-start.13 = (bf16[2,64,128]{2,1,0:T(8,128)(2,1)S(1)}, bf16[2,64,128]{2,1,0:T(8,128)(2,1)S(1)}, u32[]{:S(2)}, u32[]{:S(2)}) collective-permute-start(bf16[2,64,128]{2,1,0:T(8,128)(2,1)S(1)} %gather_fusion.17), channel_id=1, source_target_pairs={{0,16},{16,0},{8,24},{24,8},{32,48},{48,32},{40,56},{56,40},{64,80... | collective-permute-start | bytes 98312 | tf_op jit(solution)/shard_map/ppermute | solution.py:48
  98.1 16.9 %collective-permute-start.14 = (bf16[2,64,128]{2,1,0:T(8,128)(2,1)S(1)}, bf16[2,64,128]{2,1,0:T(8,128)(2,1)}, u32[]{:S(2)}, u32[]{:S(2)}) collective-permute-start(bf16[2,64,128]{2,1,0:T(8,128)(2,1)S(1)} %gather_fusion.18), channel_id=1, source_target_pairs={{0,32},{32,0},{8,40},{40,8},{16,48},{48,16},{24,56},{56,24},{64,96... | collective-permute-start | bytes 98312 | tf_op jit(solution)/shard_map/ppermute | solution.py:48
  102.2 12.8 %collective-permute-start.15 = (bf16[2,64,128]{2,1,0:T(8,128)(2,1)S(1)}, bf16[2,64,128]{2,1,0:T(8,128)(2,1)}, u32[]{:S(2)}, u32[]{:S(2)}) collective-permute-start(bf16[2,64,128]{2,1,0:T(8,128)(2,1)S(1)} %gather_fusion.19), channel_id=1, source_target_pairs={{0,64},{64,0},{8,72},{72,8},{16,80},{80,16},{24,88},{88,24},{32,96... | collective-permute-start | bytes 98312 | tf_op jit(solution)/shard_map/ppermute | solution.py:48
  112.8 2.2 %copy-start.17 = (bf16[8,64,64]{2,1,0:T(8,128)(2,1)S(1)}, bf16[8,64,64]{2,1,0:T(8,128)(2,1)}, u32[]{:S(2)}) copy-start(bf16[8,64,64]{2,1,0:T(8,128)(2,1)} %param.25) | copy-start | bytes 196612
  116.7 18.2 %copy-start.19 = (s32[32,1]{0,1:T(1,128)S(1)}, s32[32,1]{0,1:T(1,128)}, u32[]{:S(2)}) copy-start(s32[32,1]{0,1:T(1,128)} %param.26) | copy-start | bytes 388
  116.7 18.3 %copy-start.20 = (s32[32]{0:T(128)S(1)}, s32[32]{0:T(128)}, u32[]{:S(2)}) copy-start(s32[32]{0:T(128)} %param.27) | copy-start | bytes 388
  120.2 37.3 %copy-start.1 = (bf16[32,64,128]{2,1,0:T(8,128)(2,1)}, bf16[32,64,128]{2,1,0:T(8,128)(2,1)S(1)}, u32[]{:S(2)}) copy-start(bf16[32,64,128]{2,1,0:T(8,128)(2,1)S(1)} %fusion.20) | copy-start | bytes 1572868
  122.5 32.8 %collective-permute-start.16 = (bf16[2,64,128]{2,1,0:T(8,128)(2,1)S(1)}, bf16[2,64,128]{2,1,0:T(8,128)(2,1)S(1)}, u32[]{:S(2)}, u32[]{:S(2)}) collective-permute-start(bf16[2,64,128]{2,1,0:T(8,128)(2,1)S(1)} %gather_fusion.21), channel_id=1, source_target_pairs={{0,8},{8,0},{16,24},{24,16},{32,40},{40,32},{48,56},{56,48},{64,72... | collective-permute-start | bytes 98312 | tf_op jit(solution)/shard_map/ppermute | solution.py:48
  124.4 32.2 %collective-permute-start.17 = (bf16[2,64,128]{2,1,0:T(8,128)(2,1)S(1)}, bf16[2,64,128]{2,1,0:T(8,128)(2,1)S(1)}, u32[]{:S(2)}, u32[]{:S(2)}) collective-permute-start(bf16[2,64,128]{2,1,0:T(8,128)(2,1)S(1)} %gather_fusion.22), channel_id=1, source_target_pairs={{0,16},{16,0},{8,24},{24,8},{32,48},{48,32},{40,56},{56,40},{64,80... | collective-permute-start | bytes 98312 | tf_op jit(solution)/shard_map/ppermute | solution.py:48
  127.1 29.6 %collective-permute-start.18 = (bf16[2,64,128]{2,1,0:T(8,128)(2,1)S(1)}, bf16[2,64,128]{2,1,0:T(8,128)(2,1)S(1)}, u32[]{:S(2)}, u32[]{:S(2)}) collective-permute-start(bf16[2,64,128]{2,1,0:T(8,128)(2,1)S(1)} %gather_fusion.23), channel_id=1, source_target_pairs={{0,32},{32,0},{8,40},{40,8},{16,48},{48,16},{24,56},{56,24},{64,96... | collective-permute-start | bytes 98312 | tf_op jit(solution)/shard_map/ppermute | solution.py:48
  129.8 26.8 %collective-permute-start.19 = (bf16[2,64,128]{2,1,0:T(8,128)(2,1)S(1)}, bf16[2,64,128]{2,1,0:T(8,128)(2,1)S(1)}, u32[]{:S(2)}, u32[]{:S(2)}) collective-permute-start(bf16[2,64,128]{2,1,0:T(8,128)(2,1)S(1)} %gather_fusion.24), channel_id=1, source_target_pairs={{0,64},{64,0},{8,72},{72,8},{16,80},{80,16},{24,88},{88,24},{32,96... | collective-permute-start | bytes 98312 | tf_op jit(solution)/shard_map/ppermute | solution.py:48
  153.2 3.5 %copy-start.18 = (bf16[8,64,64]{2,1,0:T(8,128)(2,1)S(1)}, bf16[8,64,64]{2,1,0:T(8,128)(2,1)}, u32[]{:S(2)}) copy-start(bf16[8,64,64]{2,1,0:T(8,128)(2,1)} %param.25) | copy-start | bytes 196612
  155.3 22.3 %collective-permute-start.28 = (bf16[2,64,128]{2,0,1:T(2,128)(2,1)S(1)}, bf16[2,64,128]{2,0,1:T(2,128)(2,1)S(1)}, u32[]{:S(2)}, u32[]{:S(2)}) collective-permute-start(bf16[2,64,128]{2,0,1:T(2,128)(2,1)S(1)} %get-tuple-element.38), channel_id=1, source_target_pairs={{1,0},{2,1},{3,2},{4,3},{5,4},{6,5},{7,6},{9,8},{10,9},{11,10},{12... | collective-permute-start | bytes 98312 | tf_op jit(solution)/shard_map/ppermute | solution.py:59
  157.5 7.8 %copy-start.12 = (f32[32,64]{1,0:T(8,128)S(1)}, f32[32,64]{1,0:T(8,128)}, u32[]{:S(2)}) copy-start(f32[32,64]{1,0:T(8,128)} %param.35) | copy-start | bytes 24580
  157.5 7.9 %copy-start.9 = (bf16[4,64,64]{2,1,0:T(8,128)(2,1)S(1)}, bf16[4,64,64]{2,1,0:T(8,128)(2,1)}, u32[]{:S(2)}) copy-start(bf16[4,64,64]{2,1,0:T(8,128)(2,1)} %param.32) | copy-start | bytes 98308
  160.6 14.0 %collective-permute-start.20 = (bf16[32,64,128]{2,1,0:T(8,128)(2,1)S(1)}, bf16[32,64,128]{2,1,0:T(8,128)(2,1)S(1)}, u32[]{:S(2)}, u32[]{:S(2)}) collective-permute-start(bf16[32,64,128]{2,1,0:T(8,128)(2,1)S(1)} %fusion.17), channel_id=1, source_target_pairs={{0,1},{1,2},{2,3},{3,4},{4,5},{5,6},{6,7},{7,0},{8,9},{9,10},{10,1... | collective-permute-start | bytes 1572872 | tf_op jit(solution)/shard_map/ppermute | solution.py:22
  165.5 13.9 %collective-permute-start.21 = (bf16[32,64,128]{2,1,0:T(8,128)(2,1)S(1)}, bf16[32,64,128]{2,1,0:T(8,128)(2,1)S(1)}, u32[]{:S(2)}, u32[]{:S(2)}) collective-permute-start(bf16[32,64,128]{2,1,0:T(8,128)(2,1)S(1)} %fusion.17), channel_id=1, source_target_pairs={{0,7},{1,0},{2,1},{3,2},{4,3},{5,4},{6,5},{7,6},{8,15},{9,8},{10,9... | collective-permute-start | bytes 1572872 | tf_op jit(solution)/shard_map/ppermute | solution.py:29
  174.6 13.0 %collective-permute-start.22 = (bf16[32,64,128]{2,1,0:T(8,128)(2,1)S(1)}, bf16[32,64,128]{2,1,0:T(8,128)(2,1)S(1)}, u32[]{:S(2)}, u32[]{:S(2)}) collective-permute-start(bf16[32,64,128]{2,1,0:T(8,128)(2,1)S(1)} %collective-permute-done.20), channel_id=1, source_target_pairs={{0,1},{1,2},{2,3},{3,4},{4,5},{5,6},{6,7},{7,0},{8,9},{9,10},{10,1... | collective-permute-start | bytes 1572872 | tf_op jit(solution)/shard_map/ppermute | solution.py:22
  179.4 11.9 %collective-permute-start.23 = (bf16[32,64,128]{2,1,0:T(8,128)(2,1)S(1)}, bf16[32,64,128]{2,1,0:T(8,128)(2,1)S(1)}, u32[]{:S(2)}, u32[]{:S(2)}) collective-permute-start(bf16[32,64,128]{2,1,0:T(8,128)(2,1)S(1)} %collective-permute-done.21), channel_id=1, source_target_pairs={{0,7},{1,0},{2,1},{3,2},{4,3},{5,4},{6,5},{7,6},{8,15},{9,8},{10,9... | collective-permute-start | bytes 1572872 | tf_op jit(solution)/shard_map/ppermute | solution.py:29
  187.6 12.5 %collective-permute-start.24 = (bf16[32,64,128]{2,1,0:T(8,128)(2,1)S(1)}, bf16[32,64,128]{2,1,0:T(8,128)(2,1)S(1)}, u32[]{:S(2)}, u32[]{:S(2)}) collective-permute-start(bf16[32,64,128]{2,1,0:T(8,128)(2,1)S(1)} %collective-permute-done.22), channel_id=1, source_target_pairs={{0,1},{1,2},{2,3},{3,4},{4,5},{5,6},{6,7},{7,0},{8,9},{9,10},{10,1... | collective-permute-start | bytes 1572872 | tf_op jit(solution)/shard_map/ppermute | solution.py:22
  191.4 11.6 %collective-permute-start.25 = (bf16[32,64,128]{2,1,0:T(8,128)(2,1)S(1)}, bf16[32,64,128]{2,1,0:T(8,128)(2,1)S(1)}, u32[]{:S(2)}, u32[]{:S(2)}) collective-permute-start(bf16[32,64,128]{2,1,0:T(8,128)(2,1)S(1)} %collective-permute-done.23), channel_id=1, source_target_pairs={{0,7},{1,0},{2,1},{3,2},{4,3},{5,4},{6,5},{7,6},{8,15},{9,8},{10,9... | collective-permute-start | bytes 1572872 | tf_op jit(solution)/shard_map/ppermute | solution.py:29
  196.6 16.2 %copy-start.5 = (bf16[32,64,128]{2,1,0:T(8,128)(2,1)S(1)}, bf16[32,64,128]{2,1,0:T(8,128)(2,1)}, u32[]{:S(2)}) copy-start(bf16[32,64,128]{2,1,0:T(8,128)(2,1)} %param.28) | copy-start | bytes 1572868
  196.6 16.2 %copy-start.6 = (f32[32,64,128]{2,0,1:T(8,128)S(1)}, f32[32,64,128]{2,0,1:T(8,128)}, u32[]{:S(2)}) copy-start(f32[32,64,128]{2,0,1:T(8,128)} %fusion.78) | copy-start | bytes 3145732
  200.1 12.3 %collective-permute-start.26 = (bf16[32,64,128]{2,1,0:T(8,128)(2,1)S(1)}, bf16[32,64,128]{2,1,0:T(8,128)(2,1)S(1)}, u32[]{:S(2)}, u32[]{:S(2)}) collective-permute-start(bf16[32,64,128]{2,1,0:T(8,128)(2,1)S(1)} %collective-permute-done.24), channel_id=1, source_target_pairs={{0,1},{1,2},{2,3},{3,4},{4,5},{5,6},{6,7},{7,0},{8,9},{9,10},{10,1... | collective-permute-start | bytes 1572872 | tf_op jit(solution)/shard_map/ppermute | solution.py:22
  (2 other events, 3.0 us)
